TPU v7x, 128 devices: a whole 4x4x4 slice. The times are simulated.
128 devices in a mesh: label: 16 (over z, y_lo, core), dp: 8 (over y_hi, x).
Axes of the slice: x: 4, y: 4 (y_hi: 2, y_lo: 2; y = y_hi * 2 + y_lo), z: 4, core: 2. Of those that a mesh axis runs over, the one named last changes fastest.
Arguments:
- hidden_in: bfloat16 [16384, 768], P(('dp', 'label')), may hold values from -6 to 6
- norm_gain: float32 [768], replicated, may hold values from 0.25 to 1.75
- w_in: bfloat16 [768, 3072], replicated, may hold values from -0.21875 to 0.21875
- w_out: bfloat16 [3072, 768], replicated, may hold values from -0.15625 to 0.15625
- classifier: bfloat16 [32768, 768], P('label'), may hold values from -0.21875 to 0.21875
- centroids: bfloat16 [512, 768], P('label'), may hold values from -0.21875 to 0.21875
- radii: float32 [512], P('label'), may hold values from 0.005 to 0.08
- shortlist: int32 [16384, 16], P('dp'), may hold values from 0 to 511, all different within a row; in each aligned block of 2048 rows (0 to 2047, 2048 to 4095, ...) at most 80 rows name the same one
- positives: int32 [16384, 4], P('dp'), may hold values from 0 to 1023
- block_slot: int32 [512], replicated, may hold values from 0 to 511, each once
Outputs:
- bound_top: float32 [16384], P('dp')
- loss: float32 [16384], P(('dp', 'label'))
- query_grad: bfloat16 [16384, 768], P(('dp', 'label'))
- class_grad: bfloat16 [32768, 768], P(('label', 'dp'))
Inputs may be any that keep to these rules, and one draw needn't show every extreme that they name: `shortlist`: each query names 16 different blocks; among the 2048 queries of each data group no block is named by more than 80 queries, and some block by exactly 80; every block is named somewhere. `block_slot`: each slot once.
All inputs are finite; a program needn't handle non-finite values.
Results may differ from a plain program's by a relative error of at most 0.019.
Values may be sent and summed in bfloat16 or wider, within the bound.
No kernel may reach another device: no remote copies, remote signals or barrier semaphores. Data moves between devices by JAX's collectives and lax.ppermute only.
A program may use at most 128 MiB of HBM per device.

v0:
```python
import jax
import jax.numpy as jnp
from jax import lax
from jax.sharding import PartitionSpec as P

QCAP = 80


def encode(hidden_in, norm_gain, w_in, w_out):
    values = hidden_in.astype(jnp.float32)
    meansq = jnp.mean(values * values, axis=-1, keepdims=True)
    normed = (values * lax.rsqrt(meansq + 1e-06) * norm_gain).astype(jnp.bfloat16)
    active = jax.nn.gelu(
        jnp.dot(normed, w_in, preferred_element_type=jnp.float32), approximate=True
    ).astype(jnp.bfloat16)
    return (values + jnp.dot(active, w_out, preferred_element_type=jnp.float32)).astype(
        jnp.bfloat16
    )


def on_device(
    hidden_in,
    norm_gain,
    w_in,
    w_out,
    classifier,
    centroids,
    radii,
    shortlist,
    positives,
    block_slot,
):
    encoded = encode(hidden_in, norm_gain, w_in, w_out)
    queries = lax.all_gather(encoded, "label", axis=0, tiled=True)
    group_rows = queries.shape[0]
    width = queries.shape[1]
    local_blocks = centroids.shape[0]
    per_query = shortlist.shape[1]
    block_size = classifier.shape[0] // local_blocks
    positive_count = positives.shape[1]
    qvalues = queries.astype(jnp.float32)
    norms = jnp.sqrt(jnp.sum(qvalues * qvalues, axis=-1))
    scores = (
        jnp.dot(queries, centroids.T, preferred_element_type=jnp.float32)
        + norms[:, None] * radii[None, :]
    )
    bound_top = lax.pmax(jnp.max(scores, axis=-1), "label")
    label_idx = lax.axis_index("label")
    slots = block_slot[shortlist].reshape(-1)
    local_slot = slots - label_idx * local_blocks
    sort_key = jnp.where((local_slot >= 0) & (local_slot < local_blocks), local_slot, local_blocks)
    order = jnp.argsort(sort_key, stable=True)
    sorted_key = sort_key[order]
    every = jnp.arange(local_blocks, dtype=jnp.int32)
    first = jnp.searchsorted(sorted_key, every, side="left")
    last = jnp.searchsorted(sorted_key, every, side="right")
    offsets = jnp.arange(QCAP, dtype=jnp.int32)
    valid_flags = offsets[None, :] < (last - first)[:, None]
    pairs = order[jnp.minimum(first[:, None] + offsets[None, :], group_rows * per_query - 1)]
    rows = pairs // per_query
    which = pairs % per_query
    query_ids = jnp.arange(group_rows, dtype=jnp.int32)
    selector = (rows[:, :, None] == query_ids[None, None, :]).astype(jnp.bfloat16)
    chosen_labels = jnp.einsum(
        "mrq,qc->mrc", selector, queries, preferred_element_type=jnp.float32
    ).astype(jnp.bfloat16)
    pos_parts = jnp.concatenate([positives // 32, positives % 32], axis=1).astype(jnp.bfloat16)
    picked = jnp.einsum(
        "mrq,qp->mrp", selector, pos_parts, preferred_element_type=jnp.float32
    ).astype(jnp.int32)
    posv = picked[:, :, :positive_count] * 32 + picked[:, :, positive_count:]
    label_weights = classifier.reshape(local_blocks, block_size, width)
    label_logits = jnp.einsum(
        "mrc,mnc->mrn", chosen_labels, label_weights, preferred_element_type=jnp.float32
    )
    inner = jnp.arange(block_size, dtype=jnp.int32)
    wanted = which[:, :, None] * block_size + inner[None, None, :]
    target_labels = jnp.zeros(wanted.shape, jnp.float32)
    for index_p in range(positive_count):
        target_labels = jnp.maximum(
            target_labels, (posv[:, :, index_p][:, :, None] == wanted).astype(jnp.float32)
        )
    valid_mask = valid_flags.astype(jnp.float32)[:, :, None]
    shortlist_entry = jnp.sum(
        (jax.nn.softplus(label_logits) - target_labels * label_logits) * valid_mask, axis=-1
    )
    logit_slope = ((jax.nn.sigmoid(label_logits) - target_labels) * valid_mask).astype(jnp.bfloat16)
    weight_gradient = jnp.einsum(
        "wzv,wzc->wvc", logit_slope, chosen_labels, preferred_element_type=jnp.float32
    ).reshape(local_blocks * block_size, width)
    spread_slope = jnp.einsum(
        "mrq,mrn->qmn", selector, logit_slope, preferred_element_type=jnp.float32
    ).astype(jnp.bfloat16)
    grads = jnp.dot(
        spread_slope.reshape(group_rows, local_blocks * block_size),
        classifier,
        preferred_element_type=jnp.float32,
    ).astype(jnp.bfloat16)
    losses = jnp.einsum(
        "mrq,mr->q", selector.astype(jnp.float32), shortlist_entry, precision=lax.Precision.HIGHEST
    )
    query_total = lax.psum_scatter(grads, "label", scatter_dimension=0, tiled=True).astype(
        jnp.float32
    )
    loss_total = lax.psum_scatter(losses, "label", scatter_dimension=0, tiled=True)
    query_total, loss = (query_total, loss_total)
    class_total = lax.psum_scatter(
        weight_gradient.astype(jnp.bfloat16), "dp", scatter_dimension=0, tiled=True
    )
    return (bound_top, loss, query_total.astype(jnp.bfloat16), class_total)


def solution(mesh):
    placed = (
        P(("dp", "label"), None),
        P(),
        P(),
        P(),
        P("label", None),
        P("label", None),
        P("label"),
        P("dp", None),
        P("dp", None),
        P(),
    )
    return jax.shard_map(
        on_device,
        mesh=mesh,
        in_specs=placed,
        out_specs=(P("dp"), P(("dp", "label")), P(("dp", "label"), None), P(("label", "dp"), None)),
        check_vma=False,
    )
```

profile of v0, /device:TPU:0, one launch (start us, length us, event | category | flops | bytes accessed | tf_op | source)
XLA Modules:
  0.0 773.5 jit_solution(5631686901408259377)
XLA Ops:
  7.2 1.2 fusion.41
  8.4 6.4 fusion.29
  15.0 1.3 copy.15
  16.3 1.5 reshape.149
  17.9 345.1 %gather_fusion.2 = s32[32768]{0:T(1024)} fusion(s32[512]{0:T(512)S(1)} %copy-done.1, s32[32768]{0:T(1024)S(1)} %broadcast_clamp_fusion), kind=kCustom, calls=%fused_computation.2 | custom fusion | bytes 393216 | tf_op jit(solution)/shard_map/gather | solution.py:49
  362.9 0.9 and_select_fusion
  363.9 11.2 %sort.17 = (s32[32768]{0:T(1024)}, s32[32768]{0:T(1024)S(1)}) sort(s32[32768]{0:T(1024)S(1)} %and_select_fusion, s32[32768]{0:T(1024)S(1)} %iota.27), dimensions={0}, to_apply=%region_4.5 | sort | flops 491520 | bytes 524288 | tf_op jit(solution)/shard_map/jit(argsort)/sort | solution.py:52
  375.1 0.7 fusion.54
  375.8 180.8 %gather_fusion.3 = s32[32768]{0:T(1024)S(1)} fusion(s32[32768]{0:T(1024)S(1)} %and_select_fusion, s32[32768]{0:T(1024)} %fusion.54), kind=kCustom, calls=%fused_computation.3 | custom fusion | bytes 393216 | tf_op jit(solution)/shard_map/gather | solution.py:53
  556.6 12.0 %while.49 = (s32[]{:T(128)}, u32[32]{0:T(128)S(1)}, u32[32]{0:T(128)S(1)}, s32[32768]{0:T(1024)S(1)}, s32[]{:T(128)}, /*index=5*/s32[]{:T(128)}, s32[]{}) while((s32[]{:T(128)}, u32[32]{0:T(128)S(1)}, u32[32]{0:T(128)S(1)}, s32[32768]{0:T(1024)S(1)}, s32[]{:T(128)}, /*index=5*/s32[]{:T(128)}, s32[]{}) %tuple.86), condition=%wide.region_8.9_spmd.clone, body=%wide.region_7.8_spmd.clone.sunk | while | flops 1444 | bytes 5732 | solution.py:56
  556.6 0.7 gather_fusion.1
  557.4 0.7 gather_fusion.1
  558.1 0.7 gather_fusion.1
  558.9 0.7 gather_fusion.1
  559.6 0.7 gather_fusion.1
  560.4 0.7 gather_fusion.1
  561.1 0.7 gather_fusion.1
  561.9 0.7 gather_fusion.1
  562.6 0.7 gather_fusion.1
  563.4 0.7 gather_fusion.1
  564.2 0.7 gather_fusion.1
  564.9 0.7 gather_fusion.1
  565.7 0.7 gather_fusion.1
  566.4 0.7 gather_fusion.1
  567.2 0.7 gather_fusion.1
  567.9 0.7 gather_fusion.1
  568.7 12.0 %while.48 = (s32[]{:T(128)}, u32[32]{0:T(128)S(1)}, u32[32]{0:T(128)S(1)}, s32[32768]{0:T(1024)S(1)}, s32[]{:T(128)}, /*index=5*/s32[]{:T(128)}, s32[]{}) while((s32[]{:T(128)}, u32[32]{0:T(128)S(1)}, u32[32]{0:T(128)S(1)}, s32[32768]{0:T(1024)S(1)}, s32[]{:T(128)}, /*index=5*/s32[]{:T(128)}, s32[]{}) %tuple.84), condition=%wide.region_6.7_spmd.clone, body=%wide.region_5.6_spmd.clone.sunk | while | flops 1444 | bytes 5732 | solution.py:55
  568.7 0.7 gather_fusion
  569.4 0.7 gather_fusion
  570.2 0.7 gather_fusion
  570.9 0.7 gather_fusion
  571.7 0.7 gather_fusion
  572.5 0.7 gather_fusion
  573.2 0.7 gather_fusion
  574.0 0.7 gather_fusion
  574.7 0.7 gather_fusion
  575.5 0.7 gather_fusion
  576.2 0.7 gather_fusion
  577.0 0.7 gather_fusion
  577.7 0.7 gather_fusion
  578.5 0.7 gather_fusion
  579.2 0.7 gather_fusion
  580.0 0.7 gather_fusion
  580.7 0.1 compare_select_fusion.2
  580.8 0.1 reshape.165
  580.9 14.1 %gather_fusion.4 = s32[2560]{0:T(1024)S(1)} fusion(s32[32768]{0:T(1024)S(1)} %get-tuple-element.135, s32[3072]{0:T(1024)S(1)} %pad_clamp_fusion.2), kind=kCustom, calls=%fused_computation.4 | custom fusion | bytes 30720 | tf_op jit(solution)/shard_map/gather | solution.py:59
  595.0 0.1 reshape.164
  595.1 0.1 fusion.62
  595.2 0.1 fusion.55
  595.3 3.8 fusion.31
  599.3 11.3 %fusion.18 = bf16[32,80,768]{2,1,0:T(8,128)(2,1)S(1)} fusion(bf16[2048,768]{1,0:T(8,128)(2,1)} %all-gather.2.cloned.1.call-done, s32[32,80]{1,0:T(8,128)S(1)} %get-tuple-element.199), kind=kOutput, calls=%fused_computation.34 | convolution fusion | flops 8060272640 | bytes 7088128 | tf_op jit(solution)/shard_map/mrq,qc->mrc/dot_general | solution.py:64
  610.6 1.2 convert_reduce_fusion
  611.9 2.8 convolution_convert_fusion.1
  614.7 7.1 fusion.16
  621.8 8.4 %convolution_convert_fusion = bf16[2048,768]{1,0:T(8,128)(2,1)} fusion(bf16[2048,2048]{0,1:T(8,128)(2,1)S(1)} %bitcast.50, bf16[2048,768]{1,0:T(8,128)(2,1)S(1)} %copy-done), kind=kOutput, calls=%fused_computation.32 | convolution fusion | flops 6444023808 | bytes 14680064 | tf_op jit(solution)/shard_map/dot_general | solution.py:94
  630.3 0.6 dynamic-slice
  631.6 2.6 multiply_reduce_fusion
  634.2 2.5 multiply_reduce_fusion.1
  636.7 6.6 fusion.9
  643.3 32.3 %all-reduce = f32[2048]{0:T(1024)S(1)} all-reduce(f32[2048]{0:T(1024)S(1)} %bitcast.49), channel_id=2, replica_groups=mesh['label'=16,'dp'=8] {'label'}, use_global_device_ids=true, to_apply=%region_10.11.clone | all-reduce | flops 2048 | bytes 16384
  675.6 0.6 dynamic-slice.1
  676.2 2.9 fusion.30
  679.1 28.4 %pmax.7 = f32[2048]{0:T(1024)} all-reduce(f32[2048]{0:T(1024)S(1)} %fusion.30), channel_id=1, replica_groups=mesh['label'=16,'dp'=8] {'label'}, use_global_device_ids=true, to_apply=%region_3.0 | all-reduce | flops 2048 | bytes 16384 | tf_op jit(solution)/shard_map/pmax | solution.py:47
  707.5 59.2 %reduce-scatter.3.cloned.1.call-done = bf16[128,768]{1,0:T(8,128)(2,1)} async-done(((bf16[2048,768]{1,0:T(8,128)(2,1)}), bf16[128,768]{1,0:T(8,128)(2,1)}) %reduce-scatter.3.cloned.1.call-update) | async-done | bytes 196624 | tf_op jit(solution)/shard_map/reduce_scatter | solution.py:102
  (143 shorter events, 1.3 us)
Async XLA Ops:
  7.2 603.4 %copy-start = (bf16[2048,768]{1,0:T(8,128)(2,1)S(1)}, bf16[2048,768]{1,0:T(8,128)(2,1)}, u32[]{:S(2)}) copy-start(bf16[2048,768]{1,0:T(8,128)(2,1)} %param.18) | copy-start | bytes 9437188
  7.2 592.1 %all-gather.2.cloned.1.call-start = ((), (), s32[]{:S(2)}) async-start(), calls=%async_computation.2 | async-start | bytes 3342336 | tf_op jit(solution)/shard_map/all_gather | solution.py:34
  8.4 6.5 copy-start.3
  14.8 3.0 copy-start.1
  14.8 692.7 %reduce-scatter.5.cloned.1.call-start = ((), (), s32[]{:S(2)}) async-start(), calls=%async_computation.4 | async-start | bytes 3538944 | tf_op jit(solution)/shard_map/reduce_scatter | solution.py:107
  375.8 180.8 %copy-start.6 = (u32[32]{0:T(128)S(1)}, u32[32]{0:T(128)}, u32[]{:S(2)}) copy-start(u32[32]{0:T(128)} %custom-call.3) | copy-start | bytes 388
  375.8 180.8 %copy-start.7 = (u32[32]{0:T(128)S(1)}, u32[32]{0:T(128)}, u32[]{:S(2)}) copy-start(u32[32]{0:T(128)} %custom-call.2) | copy-start | bytes 388
  375.8 192.9 %copy-start.4 = (u32[32]{0:T(128)S(1)}, u32[32]{0:T(128)}, u32[]{:S(2)}) copy-start(u32[32]{0:T(128)} %custom-call.1) | copy-start | bytes 388
  375.8 192.9 %copy-start.5 = (u32[32]{0:T(128)S(1)}, u32[32]{0:T(128)}, u32[]{:S(2)}) copy-start(u32[32]{0:T(128)} %custom-call) | copy-start | bytes 388
  580.9 14.3 %copy-start.9 = (s32[2048,4]{0,1:T(4,128)S(1)}, s32[2048,4]{0,1:T(4,128)}, u32[]{:S(2)}) copy-start(s32[2048,4]{0,1:T(4,128)} %param.22) | copy-start | bytes 98308
  611.8 2.8 copy-start.2
  614.6 152.1 %reduce-scatter.3.cloned.1.call-start = ((), (), s32[]{:S(2)}) async-start(), calls=%async_computation.3 | async-start | bytes 3342336 | tf_op jit(solution)/shard_map/reduce_scatter | solution.py:102
  621.8 8.5 %copy-start.11 = (u32[128]{0:T(128)S(1)}, u32[128]{0:T(128)}, u32[]{:S(2)}) copy-start(u32[128]{0:T(128)} %constant.154) | copy-start | bytes 1540
  634.2 42.0 %copy-start.8 = (bf16[32,768]{1,0:T(8,128)(2,1)S(1)}, bf16[32,768]{1,0:T(8,128)(2,1)}, u32[]{:S(2)}) copy-start(bf16[32,768]{1,0:T(8,128)(2,1)} %param.19) | copy-start | bytes 147460
  634.2 42.0 %copy-start.10 = (f32[32]{0:T(128)S(1)}, f32[32]{0:T(128)}, u32[]{:S(2)}) copy-start(f32[32]{0:T(128)} %param.20) | copy-start | bytes 388
Sparse Core Ops, SparseCore 0:
  15.0 38.5 all-gather.1
  614.8 82.9 reduce-scatter.4
  700.9 65.8 reduce-scatter.2
where the time goes:
time: 778 us; the launch traced here: 774 us
  local copies, waits for them, and re-layouts  567 us (73%)
  blocking collectives  60.7 us (8%)
  waiting for transfers between devices  59.3 us (8%)
  matrix products  50.6 us (7%)
  other arithmetic  20.3 us (3%)
  between operations  15 us (2%)
    gather x1, local copies, waits for them, and re-layouts, on_device(): slots = block_slot[shortlist].reshape(-1)  345 us
    gather x1, local copies, waits for them, and re-layouts, on_device(): sorted_key = sort_key[order]  181 us
    reduce_scatter x1, waiting for transfers between devices, on_device(): lax.psum_scatter(grads, 'label', scatter_dimension=0, tiled=True)  59.2 us
    unnamed x1, blocking collectives  32.3 us
    pmax x1, blocking collectives, on_device(): bound_top = lax.pmax(jnp.max(scores, axis=-1), 'label')  28.4 us
  transfers between devices with their start and end apart: 3, of which 1 were waited for; matrix products, arithmetic and copies ran while one was open for 79% of the time, Pallas kernels for 0%

commit v1 on v0

v1 whole, which is shorter than its diff:
```python
import functools

import jax
import jax.numpy as jnp
from jax import lax
from jax.experimental import pallas as pl
from jax.experimental.pallas import tpu as pltpu
from jax.sharding import PartitionSpec as P

F32 = jnp.float32
BF16 = jnp.bfloat16

NZ, NY, NC = 4, 2, 2
NX, NYH = 4, 2
ROWS = 128
PLANE = ROWS * NY * NC
EXTRA = 16
D = 768
BL = 64
K = 16
P_SIZE = 4
LBLK = 32
LOCAL = LBLK * BL
BLOCKS = 512
TILE = 512
SLOTS = TILE // BL
CROWS = 48
OUTSIDE = -1e30
MIB = 1024 * 1024

DP_ORDER = ((2, 1), (1, 1), (3, 1), (2, 0), (1, 0), (3, 0), (0, 1), (0, 0))


def label_perm(dz, dy, dc):
    at = lambda z, y, c: (z % NZ) * 4 + (y % NY) * 2 + c % NC
    return [
        (at(z, y, c), at(z + dz, y + dy, c + dc))
        for z in range(NZ)
        for y in range(NY)
        for c in range(NC)
    ]


def dp_perm(dx, dy):
    at = lambda x, y: (y % NYH) * 4 + x % NX
    return [(at(x, y), at(x + dx, y + dy)) for y in range(NYH) for x in range(NX)]


def send_label(x, dz, dy, dc):
    return lax.ppermute(x, "label", label_perm(dz, dy, dc))


def vmem(*shape):
    return pl.BlockSpec(memory_space=pltpu.VMEM)


def params(limit=48):
    return pltpu.CompilerParams(vmem_limit_bytes=limit * MIB)


def cost(us):
    return pl.CostEstimate(flops=int(us * 8e8), bytes_accessed=int(us * 1e5), transcendentals=0)


def encode(hidden_in, norm_gain, w_in, w_out):
    values = hidden_in.astype(F32)
    meansq = jnp.mean(values * values, axis=-1, keepdims=True)
    normed = (values * lax.rsqrt(meansq + 1e-06) * norm_gain).astype(BF16)
    active = jax.nn.gelu(
        jnp.dot(normed, w_in, preferred_element_type=F32), approximate=True
    ).astype(BF16)
    return (values + jnp.dot(active, w_out, preferred_element_type=F32)).astype(BF16)


def prepare_kernel(me_ref, sl_ref, pos_ref, bs_ref, neg_ref, wa_ref, wb_ref):
    me = me_ref[0]
    z, low = me // 4, me % 4
    slot_rows = lax.broadcasted_iota(jnp.int32, (LBLK, BLOCKS), 0) + me * LBLK
    ids = lax.broadcasted_iota(jnp.int32, (LBLK, BLOCKS), 1).astype(F32)
    here = jnp.sum(jnp.where(bs_ref[...] == slot_rows, ids, 0.0), axis=1, keepdims=True)
    here = jnp.broadcast_to(here, (LBLK, ROWS))
    which = lax.broadcasted_iota(jnp.int32, (K, ROWS), 0)
    for dz in range(NZ):
        for j in range(4):
            nat = lax.rem(z + NZ - dz, NZ) * 4 + (low ^ j)
            lanes = pl.ds(pl.multiple_of(nat * ROWS, ROWS), ROWS)
            sl = sl_ref[:, lanes].astype(F32)
            pos = pos_ref[:, lanes]
            neg = jnp.full((LBLK, ROWS), OUTSIDE, F32)
            for k in range(K):
                neg = jnp.where(here == sl[k : k + 1], 0.0, neg)
            wa = jnp.zeros((LBLK, ROWS), jnp.int32)
            wb = jnp.zeros((LBLK, ROWS), jnp.int32)
            for p in range(P_SIZE):
                kp, jp = pos[p : p + 1] >> 6, pos[p : p + 1] & 63
                bid = jnp.sum(jnp.where(which == kp, sl, 0.0), axis=0, keepdims=True)
                bit = jnp.full((1, ROWS), 1, jnp.int32) << (31 - (jp & 31))
                match = here == bid
                wa = wa | jnp.where(match, jnp.where(jp < 32, bit, 0), 0)
                wb = wb | jnp.where(match, jnp.where(jp < 32, 0, bit), 0)
            out = pl.ds(j * ROWS, ROWS)
            neg_ref[dz, :, out] = neg
            wa_ref[dz, :, out] = wa
            wb_ref[dz, :, out] = wb


def prepare(me, sl, pos, bs):
    out = lambda t: jax.ShapeDtypeStruct((NZ, LBLK, PLANE), t)
    return pl.pallas_call(
        prepare_kernel,
        out_shape=(out(F32), out(jnp.int32), out(jnp.int32)),
        in_specs=[pl.BlockSpec(memory_space=pltpu.SMEM), vmem(), vmem(), vmem()],
        out_specs=(vmem(), vmem(), vmem()),
        compiler_params=params(),
        cost_estimate=cost(3),
        name="prepare",
    )(me, sl, pos, bs)


def split3(value):
    hi = value.astype(BF16)
    rest = value - hi.astype(F32)
    mid = rest.astype(BF16)
    lo = (rest - mid.astype(F32)).astype(BF16)
    return hi, mid, lo


def loss_rows(row):
    hi, mid, lo = split3(row)
    return jnp.concatenate([hi, mid, lo, jnp.zeros((EXTRA, D - 3 * ROWS), BF16)], axis=1)


def joined(rows):
    return rows[:, :ROWS] + rows[:, ROWS : 2 * ROWS] + rows[:, 2 * ROWS : 3 * ROWS]


def slope_kernel(q0, q1, q2, q3, c_ref, neg_ref, wa_ref, wb_ref, s_ref, a0_ref, a1_ref,
                 q_ref, x_ref, acc_ref, loss_ref):
    i = pl.program_id(0)

    @pl.when(i == 0)
    def _():
        for j, q in enumerate((q0, q1, q2, q3)):
            q_ref[j * ROWS : (j + 1) * ROWS, :] = q[...]
        acc_ref[...] = jnp.zeros_like(acc_ref)
        loss_ref[...] = jnp.zeros_like(loss_ref)

    x_ref[...] = lax.dot_general(
        c_ref[...], q_ref[...], (((1,), (1,)), ((), ())), preferred_element_type=F32
    )
    shift = lax.broadcasted_iota(jnp.int32, (32, ROWS), 0)
    for t in range(PLANE // ROWS):
        lanes = slice(t * ROWS, (t + 1) * ROWS)
        prod = jnp.ones((8, ROWS), F32)
        relu = jnp.zeros((8, ROWS), F32)
        for s in range(SLOTS):
            rows = slice(s * BL, (s + 1) * BL)
            x = x_ref[rows, lanes] + neg_ref[s : s + 1, lanes]
            bits = jnp.concatenate(
                [wa_ref[s : s + 1, lanes] << shift, wb_ref[s : s + 1, lanes] << shift], axis=0
            )
            hit = bits < 0
            flipped = -x
            e = jnp.exp(jnp.minimum(x, flipped))
            x = jnp.where(hit, flipped, x)
            u = 1.0 + e
            sig = jnp.where(x >= 0.0, 1.0, e) * pl.reciprocal(u, approx=True)
            s_ref[rows, lanes] = jnp.where(hit, -sig, sig).astype(BF16)
            u8 = u.reshape(8, 8, ROWS)
            r8 = jnp.maximum(x, 0.0).reshape(8, 8, ROWS)
            for n in range(8):
                prod = prod * u8[n]
                relu = relu + r8[n]
        loss_ref[:, lanes] += jnp.log(prod) + relu
    acc_ref[...] += lax.dot_general(
        s_ref[...], c_ref[...], (((0,), (0,)), ((), ())), preferred_element_type=F32
    )

    @pl.when(i == pl.num_programs(0) - 1)
    def _():
        for j in range(4):
            out, dy = (a0_ref, a1_ref)[j % 2], j // 2
            rows = slice(j * ROWS, (j + 1) * ROWS)
            out[dy, :ROWS, :] = acc_ref[rows, :].astype(BF16)
            row = jnp.sum(loss_ref[:, rows], axis=0, keepdims=True)
            out[dy, ROWS:, :] = loss_rows(jnp.broadcast_to(row, (EXTRA, ROWS)))


def slopes(plane, shards, classifier, neg, wa, wb):
    whole = pl.BlockSpec((ROWS, D), lambda i: (0, 0))
    flag = pl.BlockSpec((None, SLOTS, PLANE), lambda i: (plane, i, 0))
    part = jax.ShapeDtypeStruct((NY, ROWS + EXTRA, D), BF16)
    part_spec = pl.BlockSpec((NY, ROWS + EXTRA, D), lambda i: (0, 0, 0))
    return pl.pallas_call(
        slope_kernel,
        out_shape=(jax.ShapeDtypeStruct((LOCAL, PLANE), BF16), part, part),
        grid=(LOCAL // TILE,),
        in_specs=[whole] * 4 + [pl.BlockSpec((TILE, D), lambda i: (i, 0)), flag, flag, flag],
        out_specs=(pl.BlockSpec((TILE, PLANE), lambda i: (i, 0)), part_spec, part_spec),
        scratch_shapes=[
            pltpu.VMEM((PLANE, D), BF16),
            pltpu.VMEM((TILE, PLANE), F32),
            pltpu.VMEM((PLANE, D), F32),
            pltpu.VMEM((8, PLANE), F32),
        ],
        compiler_params=params(),
        cost_estimate=cost(7),
        name="slopes",
    )(*shards, classifier, neg, wa, wb)


def pair_kernel(a_ref, b_ref, out_ref):
    for dy in range(NY):
        out_ref[dy, :ROWS, :] = (
            a_ref[dy, :ROWS, :].astype(F32) + b_ref[dy, :ROWS, :].astype(F32)
        ).astype(BF16)
        out_ref[dy, ROWS:, :] = loss_rows(
            joined(a_ref[dy, ROWS:, :].astype(F32) + b_ref[dy, ROWS:, :].astype(F32))
        )


def pair(a, b):
    return pl.pallas_call(
        pair_kernel,
        out_shape=jax.ShapeDtypeStruct(a.shape, BF16),
        in_specs=[vmem(), vmem()],
        out_specs=vmem(),
        compiler_params=params(16),
        cost_estimate=cost(1),
        name="pair",
    )(a, b)


def across_kernel(a, b, c, d, out_ref):
    total = sum(r[1].astype(F32) for r in (a, b, c, d))
    out_ref[:ROWS, :] = total[:ROWS].astype(BF16)
    out_ref[ROWS:, :] = loss_rows(joined(total[ROWS:]))


def across(parts):
    return pl.pallas_call(
        across_kernel,
        out_shape=jax.ShapeDtypeStruct((ROWS + EXTRA, D), BF16),
        in_specs=[vmem()] * 4,
        out_specs=vmem(),
        compiler_params=params(16),
        cost_estimate=cost(1),
        name="across",
    )(*parts)


def finish_kernel(a, b, c, d, y_ref, grad_ref, loss_ref):
    total = sum(r[0].astype(F32) for r in (a, b, c, d)) + y_ref[...].astype(F32)
    grad_ref[...] = total[:ROWS].astype(BF16)
    loss_ref[...] = joined(total[ROWS : ROWS + 8])[:1]


def finish(parts, y):
    return pl.pallas_call(
        finish_kernel,
        out_shape=(
            jax.ShapeDtypeStruct((ROWS, D), BF16),
            jax.ShapeDtypeStruct((1, ROWS), F32),
        ),
        in_specs=[vmem()] * 5,
        out_specs=(vmem(), vmem()),
        compiler_params=params(16),
        cost_estimate=cost(1),
        name="finish",
    )(*parts, y)


def class_kernel(count, order_ref, *refs):
    s_refs, q_refs = refs[:NZ], refs[NZ : NZ + 16]
    outs, q_ref = refs[NZ + 16 : NZ + 16 + count], refs[-1]
    i = pl.program_id(0)

    @pl.when(i == 0)
    def _():
        for r, q in enumerate(q_refs):
            q_ref[r * ROWS : (r + 1) * ROWS, :] = q[...]

    total = sum(
        jnp.dot(
            s[...], q_ref[n * PLANE : (n + 1) * PLANE, :], preferred_element_type=F32
        )
        for n, s in enumerate(s_refs)
    ).astype(BF16)
    for n, out in enumerate(outs):

        @pl.when(i == n)
        def _():
            out[...] = total


def class_blocks(order, slope_planes, shards):
    count = order.shape[0]
    rows = LOCAL // (NX * NYH)
    return pl.pallas_call(
        functools.partial(class_kernel, count),
        out_shape=[jax.ShapeDtypeStruct((rows, D), BF16)] * count,
        grid_spec=pltpu.PrefetchScalarGridSpec(
            num_scalar_prefetch=1,
            grid=(count,),
            in_specs=[pl.BlockSpec((rows, PLANE), lambda i, o: (o[i], 0))] * NZ
            + [pl.BlockSpec((ROWS, D), lambda i, o: (0, 0))] * 16,
            out_specs=[pl.BlockSpec((rows, D), lambda i, o: (0, 0))] * count,
            scratch_shapes=[pltpu.VMEM((16 * ROWS, D), BF16)],
        ),
        compiler_params=params(),
        cost_estimate=cost(5),
        name="class_blocks",
    )(order, *slope_planes, *shards)


def bound_kernel(me_ref, cent_ref, radii_ref, *refs):
    q_refs, out_ref = refs[:16], refs[16]
    me = me_ref[0]
    for r, q in enumerate(q_refs):
        value = q[...].astype(F32)
        norm = jnp.sqrt(jnp.sum(value * value, axis=1, keepdims=True))
        score = lax.dot_general(
            q[...], cent_ref[...], (((1,), (1,)), ((), ())), preferred_element_type=F32
        )
        top = jnp.max(score + norm * radii_ref[...], axis=1, keepdims=True)
        row = jnp.broadcast_to(top, (ROWS, ROWS)).T[:1]
        nat = lax.rem(me // 4 + NZ - r // 4, NZ) * 4 + ((me % 4) ^ (r % 4))
        out_ref[:, pl.ds(pl.multiple_of(nat * ROWS, ROWS), ROWS)] = row


def bounds(me, cent, radii, shards):
    return pl.pallas_call(
        bound_kernel,
        out_shape=jax.ShapeDtypeStruct((1, 16 * ROWS), F32),
        in_specs=[pl.BlockSpec(memory_space=pltpu.SMEM)] + [vmem()] * 18,
        out_specs=vmem(),
        compiler_params=params(),
        cost_estimate=cost(4),
        name="bounds",
    )(me, cent, radii, *shards)


def on_device(
    hidden_in,
    norm_gain,
    w_in,
    w_out,
    classifier,
    centroids,
    radii,
    shortlist,
    positives,
    block_slot,
):
    label = lax.axis_index("label")
    dp = lax.axis_index("dp")
    me = label.astype(jnp.int32).reshape(1)

    hi = lax.reduce_precision(radii, 8, 7)
    mid = lax.reduce_precision(radii - hi, 8, 7)
    lo = lax.reduce_precision(radii - hi - mid, 8, 7)
    terms = jnp.stack([hi, mid, lo]).astype(BF16)
    packed = jnp.concatenate(
        [centroids, jnp.pad(terms, ((0, CROWS - LBLK - 3), (0, D - LBLK)))], axis=0
    )
    every = lax.all_gather(packed, "label", axis=0)

    neg, wa, wb = prepare(me, shortlist.T, positives.T, block_slot.reshape(1, -1))
    encoded = encode(hidden_in, norm_gain, w_in, w_out)

    held = {(0, 0, 0): encoded, (0, 1, 0): send_label(encoded, 0, 1, 0)}
    for dz in (2, 1, 3):
        held[dz, 0, 0] = send_label(encoded, dz, 0, 0)
    for dz in (2, 1, 3):
        held[dz, 1, 0] = send_label(held[0, 1, 0], dz, 0, 0)
    for dz in range(NZ):
        for dy in range(NY):
            held[dz, dy, 1] = send_label(held[dz, dy, 0], 0, 0, 1)
    planes = [[held[dz, dy, dc] for dy in range(NY) for dc in range(NC)] for dz in range(NZ)]
    shards = [q for plane in planes for q in plane]

    slope_planes = [None] * NZ
    parts = [None] * NZ
    for dz in (0, 1, 3, 2):
        slope_planes[dz], keep, give = slopes(dz, planes[dz], classifier, neg, wa, wb)
        both = pair(keep, send_label(give, 0, 0, 1))
        parts[dz] = both if dz == 0 else send_label(both, -dz, 0, 0)

    order = jnp.stack(
        [((dp // NX + dy) % NYH) * NX + (dp % NX + dx) % NX for dx, dy in DP_ORDER]
    ).astype(jnp.int32)
    blocks = class_blocks(order[:4], slope_planes, shards)
    blocks = blocks + class_blocks(order[4:], slope_planes, shards)
    class_total = blocks[-1].astype(F32)
    for (dx, dy), block in zip(DP_ORDER[:-1], blocks):
        class_total = class_total + lax.ppermute(block, "dp", dp_perm(dx, dy)).astype(F32)

    query_grad, loss = finish(parts, send_label(across(parts), 0, 1, 0))

    cent = every[:, :LBLK].reshape(BLOCKS, D)
    pieces = every[:, LBLK : LBLK + 3, :LBLK].astype(F32)
    radius = (pieces[:, 0] + pieces[:, 1] + pieces[:, 2]).reshape(1, BLOCKS)
    bound_top = bounds(me, cent, radius, shards)
    return (
        bound_top.reshape(-1),
        loss.reshape(-1),
        query_grad,
        class_total.astype(BF16),
    )


def solution(mesh):
    placed = (
        P(("dp", "label"), None),
        P(),
        P(),
        P(),
        P("label", None),
        P("label", None),
        P("label"),
        P("dp", None),
        P("dp", None),
        P(),
    )
    return jax.shard_map(
        on_device,
        mesh=mesh,
        in_specs=placed,
        out_specs=(P("dp"), P(("dp", "label")), P(("dp", "label"), None), P(("label", "dp"), None)),
        check_vma=False,
    )
```

time: 778 us -> 148 us (0.19)
  local copies, waits for them, and re-layouts: 567 us -> 9.32 us
  blocking collectives: 60.7 us -> 0 us
  Pallas kernels: 0 us -> 51.9 us
  matrix products: 50.6 us -> 5.73 us
  starting transfers between devices: 0.12 us -> 40.4 us
  waiting for transfers between devices: 59.3 us -> 22.4 us
  other arithmetic: 20.3 us -> 3.09 us
    gather x36 -> x0, local copies, waits for them, and re-layouts: 563 us -> none  [the longest x1 345 us: on_device(): slots = block_slot[shortlist].reshape(-1)]
    reduce_scatter x2 -> x0, waiting for transfers between devices: 59.2 us -> none  [the longest x1 59.2 us: on_device(): lax.psum_scatter(grads, 'label', scatter_dimension=0, tiled=True)]
    pallas_call x0 -> x14, Pallas kernels: none -> 51.9 us  [the longest x4 31.9 us: slopes(): pl.pallas_call(slope_kernel, out_shape=(jax.ShapeDtypeStruct((LOCAL, PLAN...]
    dot_general x9 -> x1, matrix products: 50.6 us -> 5.73 us  [encode(): jnp.dot(active, w_out, preferred_element_type=F32)]
    ppermute x0 -> x30, starting transfers between devices: none -> 40.3 us  [the longest x7 20.8 us: on_device(): lax.ppermute(block, 'dp', dp_perm(dx, dy)).astype(F32)]
    unnamed x1 -> x0, blocking collectives: 32.3 us -> none
    pmax x1 -> x0, blocking collectives: 28.4 us -> none  [on_device(): bound_top = lax.pmax(jnp.max(scores, axis=-1), 'label')]
    ppermute x0 -> x30, waiting for transfers between devices: none -> 22.4 us  [the longest x7 13 us: on_device(): lax.ppermute(block, 'dp', dp_perm(dx, dy)).astype(F32)]
  transfers between devices with their start and end apart: 3 -> 31, of which waited for: 1 -> 9; matrix products, arithmetic and copies ran while one was open for 79% -> 1% of each run, Pallas kernels for 0% -> 32%
where the time goes in v1:
time: 148 us; the launch traced here: 147 us
  Pallas kernels  51.9 us (35%)
  starting transfers between devices  40.4 us (27%)
  waiting for transfers between devices  22.4 us (15%)
  between operations  14.4 us (10%)
  local copies, waits for them, and re-layouts  9.32 us (6%)
  matrix products  5.73 us (4%)
  other arithmetic  3.09 us (2%)
    pallas_call x4, Pallas kernels, slopes(): pl.pallas_call(slope_kernel, out_shape=(jax.ShapeDtypeStruct((LOCAL, PLAN...  31.9 us
    ppermute x7, starting transfers between devices, on_device(): lax.ppermute(block, 'dp', dp_perm(dx, dy)).astype(F32)  20.8 us
    ppermute x23, starting transfers between devices, send_label(): return lax.ppermute(x, 'label', label_perm(dz, dy, dc))  19.5 us
    ppermute x7, waiting for transfers between devices, on_device(): lax.ppermute(block, 'dp', dp_perm(dx, dy)).astype(F32)  13 us
    pallas_call x2, Pallas kernels, class_blocks(): pl.pallas_call(functools.partial(class_kernel, count), out_shape=[jax.Sha...  12.7 us
    ppermute x23, waiting for transfers between devices, send_label(): return lax.ppermute(x, 'label', label_perm(dz, dy, dc))  9.4 us
    unnamed x26, local copies, waits for them, and re-layouts  7.29 us
    dot_general x1, matrix products, encode(): jnp.dot(active, w_out, preferred_element_type=F32)  5.73 us
  transfers between devices with their start and end apart: 31, of which 9 were waited for; matrix products, arithmetic and copies ran while one was open for 1% of the time, Pallas kernels for 32%

profile of v1, /device:TPU:0, one launch (start us, length us, event | category | flops | bytes accessed | tf_op | source)
XLA Modules:
  0.0 147.1 jit_solution(3201798989748486194)
XLA Ops:
  7.2 0.0 all-gather.3.cloned.1.call-start
  7.2 1.0 fusion.14
  8.3 0.0 copy-start.11
  8.3 0.0 copy-start.4
  8.3 0.0 copy-start.5
  8.3 5.7 %fusion.8.refs_0_.q0.refs_4_ = bf16[128,768]{1,0:T(8,128)(2,1)S(1)} fusion(bf16[3072,768]{1,0:T(8,128)(2,1)} %param.13, bf16[128,768]{1,0:T(8,128)(2,1)} %param.10, bf16[768,3072]{1,0:T(8,128)(2,1)} %param.12, f32[768]{0:T(1024)} %param.11, f32[128]{0:T(128)S(1)} %add_rsqrt_fusion), kind=kOutput, calls=%fused_computation.10 | convolution fusion | flops 1212186624 | bytes 9833984 | tf_op jit(solution)/shard_map/dot_general | solution.py:72
  14.1 4.2 %collective-permute-start.11 = (bf16[128,768]{1,0:T(8,128)(2,1)S(1)}, bf16[128,768]{1,0:T(8,128)(2,1)S(1)}, u32[]{:S(2)}, u32[]{:S(2)}) collective-permute-start(bf16[128,768]{1,0:T(8,128)(2,1)S(1)} %fusion.8.refs_0_.q0.refs_4_), channel_id=1, source_target_pairs={{0,96},{8,104},{16,112},{24,120},{32,0},{40,8},{48,16},{56,24},{64... | collective-permute-start | bytes 589832 | tf_op jit(solution)/shard_map/ppermute | solution.py:50
  18.3 1.6 %collective-permute-start.1 = (bf16[128,768]{1,0:T(8,128)(2,1)S(1)}, bf16[128,768]{1,0:T(8,128)(2,1)S(1)}, u32[]{:S(2)}, u32[]{:S(2)}) collective-permute-start(bf16[128,768]{1,0:T(8,128)(2,1)S(1)} %fusion.8.refs_0_.q0.refs_4_), channel_id=1, source_target_pairs={{0,16},{8,24},{16,0},{24,8},{32,48},{40,56},{48,32},{56,40},{64,80... | collective-permute-start | bytes 589832 | tf_op jit(solution)/shard_map/ppermute | solution.py:50
  19.9 0.6 pad_maximum_fusion
  20.5 0.0 all-gather.3.cloned.1.call-update
  20.7 0.1 pad_add_fusion.1.order_ref
  20.7 3.9 %collective-permute-done.1.refs_2_.q2.refs_6_ = bf16[128,768]{1,0:T(8,128)(2,1)S(1)} collective-permute-done((bf16[128,768]{1,0:T(8,128)(2,1)S(1)}, bf16[128,768]{1,0:T(8,128)(2,1)S(1)}, u32[]{:S(2)}, u32[]{:S(2)}) %collective-permute-start.1) | collective-permute-done | bytes 196640 | tf_op jit(solution)/shard_map/ppermute | solution.py:50
  24.6 0.7 collective-permute-start.13
  25.3 0.7 prepare.1
  26.0 1.7 %collective-permute-done.11.refs_12_.q0.refs_16_ = bf16[128,768]{1,0:T(8,128)(2,1)S(1)} collective-permute-done((bf16[128,768]{1,0:T(8,128)(2,1)S(1)}, bf16[128,768]{1,0:T(8,128)(2,1)S(1)}, u32[]{:S(2)}, u32[]{:S(2)}) %collective-permute-start.11) | collective-permute-done | bytes 196640 | tf_op jit(solution)/shard_map/ppermute | solution.py:50
  27.7 5.2 %collective-permute-start.9 = (bf16[128,768]{1,0:T(8,128)(2,1)S(1)}, bf16[128,768]{1,0:T(8,128)(2,1)S(1)}, u32[]{:S(2)}, u32[]{:S(2)}) collective-permute-start(bf16[128,768]{1,0:T(8,128)(2,1)S(1)} %collective-permute-done.1.refs_2_.q2.refs_6_), channel_id=1, source_target_pairs={{0,64},{8,72},{16,80},{24,88},{32,96},{40,104},{48,112},{56,120},{... | collective-permute-start | bytes 589832 | tf_op jit(solution)/shard_map/ppermute | solution.py:50
  32.9 0.1 collective-permute-done.13.refs_14_.q2.refs_18_
  33.0 0.5 collective-permute-start.14
  33.5 7.9 %slopes.4 = (bf16[2048,512]{1,0:T(8,128)(2,1)S(1)}, bf16[2,144,768]{2,1,0:T(8,128)(2,1)S(1)}, bf16[2,144,768]{2,1,0:T(8,128)(2,1)S(1)}) custom-call(bf16[128,768]{1,0:T(8,128)(2,1)S(1)} %fusion.8.refs_0_.q0.refs_4_, bf16[128,768]{1,0:T(8,128)(2,1)S(1)} %collective-permute-done.refs_1_.q1.refs_5_, ...), custom_call_target="tpu_custom_call" | custom-call | flops 5600000000 | bytes 700000 | tf_op jit(solution)/shard_map/slopes/pallas_call | solution.py:194
  41.4 1.3 copy-done.7
  42.8 0.1 collective-permute-start.8
  42.8 0.4 collective-permute-start.4
  43.3 0.9 collective-permute-done.9.refs_10_.q2.refs_14_
  44.2 0.5 collective-permute-start.10
  44.7 0.1 collective-permute-start.6
  44.8 7.9 %slopes.7 = (bf16[2048,512]{1,0:T(8,128)(2,1)S(1)}, bf16[2,144,768]{2,1,0:T(8,128)(2,1)S(1)}, bf16[2,144,768]{2,1,0:T(8,128)(2,1)S(1)}) custom-call(bf16[128,768]{1,0:T(8,128)(2,1)S(1)} %collective-permute-done.11.refs_12_.q0.refs_16_, bf16[128,768]{1,0:T(8,128)(2,1)S(1)} %collective-permute-done.12.refs_13_.q1.refs_17_, ...), custom_call_target="tpu_custom_call" | custom-call | flops 5600000000 | bytes 700000 | tf_op jit(solution)/shard_map/slopes/pallas_call | solution.py:194
  52.7 1.3 copy-done.8
  54.0 0.4 collective-permute-start.20
  54.5 8.0 %slopes.6 = (bf16[2048,512]{1,0:T(8,128)(2,1)S(1)}, bf16[2,144,768]{2,1,0:T(8,128)(2,1)S(1)}, bf16[2,144,768]{2,1,0:T(8,128)(2,1)S(1)}) custom-call(bf16[128,768]{1,0:T(8,128)(2,1)S(1)} %collective-permute-done.7.refs_8_.q0.refs_12_, bf16[128,768]{1,0:T(8,128)(2,1)S(1)} %collective-permute-done.8.refs_9_.q1.refs_13_, ...), custom_call_target="tpu_custom_call" | custom-call | flops 5600000000 | bytes 700000 | tf_op jit(solution)/shard_map/slopes/pallas_call | solution.py:194
  62.5 1.4 copy-done.9
  63.9 0.1 collective-permute-start.18
  63.9 8.0 %slopes.5 = (bf16[2048,512]{1,0:T(8,128)(2,1)S(1)}, bf16[2,144,768]{2,1,0:T(8,128)(2,1)S(1)}, bf16[2,144,768]{2,1,0:T(8,128)(2,1)S(1)}) custom-call(bf16[128,768]{1,0:T(8,128)(2,1)S(1)} %collective-permute-done.3.refs_4_.q0.refs_8_, bf16[128,768]{1,0:T(8,128)(2,1)S(1)} %collective-permute-done.4.refs_5_.q1.refs_9_, ...), custom_call_target="tpu_custom_call" | custom-call | flops 5600000000 | bytes 700000 | tf_op jit(solution)/shard_map/slopes/pallas_call | solution.py:194
  72.0 1.4 copy-done.10
  73.4 0.4 collective-permute-start.16
  73.8 6.4 %class_blocks.3 = (bf16[256,768]{1,0:T(8,128)(2,1)S(1)}, bf16[256,768]{1,0:T(8,128)(2,1)S(1)}, bf16[256,768]{1,0:T(8,128)(2,1)S(1)}, bf16[256,768]{1,0:T(8,128)(2,1)S(1)}) custom-call(s32[4]{0:T(128)S(1)} %pad_add_fusion.1.order_ref, bf16[2048,512]{1,0:T(8,128)(2,1)} %copy-done.7, bf16[2048,512]{1,0:T(8,128)(2,1)} %copy-done.10, ...), custom_call_target="tpu_custom_call" | custom-call | flops 4000000000 | bytes 500000 | tf_op jit(solution)/shard_map/class_blocks/pallas_call | solution.py:299
  80.2 5.7 %collective-permute-start.23 = (bf16[256,768]{1,0:T(8,128)(2,1)S(1)}, bf16[256,768]{1,0:T(8,128)(2,1)S(1)}, u32[]{:S(2)}, u32[]{:S(2)}) collective-permute-start(bf16[256,768]{1,0:T(8,128)(2,1)S(1)} %get-tuple-element.47), channel_id=1, source_target_pairs={{0,6},{1,7},{2,4},{3,5},{4,2},{5,3},{6,0},{7,1},{8,14},{9,15},{10,... | collective-permute-start | bytes 1179656 | tf_op jit(solution)/shard_map/ppermute | solution.py:396
  85.9 0.4 collective-permute-start.24
  86.2 0.1 pair.7
  86.3 1.6 %collective-permute-start.21 = (bf16[2,144,768]{2,1,0:T(8,128)(2,1)S(1)}, bf16[2,144,768]{2,1,0:T(8,128)(2,1)S(1)}, u32[]{:S(2)}, u32[]{:S(2)}) collective-permute-start(bf16[2,144,768]{2,1,0:T(8,128)(2,1)S(1)} %pair.7), channel_id=1, source_target_pairs={{0,32},{8,40},{16,48},{24,56},{32,64},{40,72},{48,80},{56,88},{64,... | collective-permute-start | bytes 1327112 | tf_op jit(solution)/shard_map/ppermute | solution.py:50
  87.9 0.1 pair.6
  88.0 3.6 %collective-permute-start.19 = (bf16[2,144,768]{2,1,0:T(8,128)(2,1)S(1)}, bf16[2,144,768]{2,1,0:T(8,128)(2,1)S(1)}, u32[]{:S(2)}, u32[]{:S(2)}) collective-permute-start(bf16[2,144,768]{2,1,0:T(8,128)(2,1)S(1)} %pair.6), channel_id=1, source_target_pairs={{0,64},{8,72},{16,80},{24,88},{32,96},{40,104},{48,112},{56,120},{... | collective-permute-start | bytes 1327112 | tf_op jit(solution)/shard_map/ppermute | solution.py:50
  91.6 0.1 pair.5
  91.8 0.2 collective-permute-start.17
  92.0 0.1 pad_add_fusion.order_ref
  92.1 6.4 %class_blocks.2 = (bf16[256,768]{1,0:T(8,128)(2,1)S(1)}, bf16[256,768]{1,0:T(8,128)(2,1)S(1)}, bf16[256,768]{1,0:T(8,128)(2,1)S(1)}, bf16[256,768]{1,0:T(8,128)(2,1)S(1)}) custom-call(s32[4]{0:T(128)S(1)} %pad_add_fusion.order_ref, bf16[2048,512]{1,0:T(8,128)(2,1)} %copy-done.7, bf16[2048,512]{1,0:T(8,128)(2,1)} %copy-done.10, bf16[2048,512]{1,0:T(8,128)(2,1)} %copy-done.9, ...), custom_call_target="tpu_custom_call" | custom-call | flops 4000000000 | bytes 500000 | tf_op jit(solution)/shard_map/class_blocks/pallas_call | solution.py:299
  98.5 5.3 %collective-permute-start.25 = (bf16[256,768]{1,0:T(8,128)(2,1)S(1)}, bf16[256,768]{1,0:T(8,128)(2,1)S(1)}, u32[]{:S(2)}, u32[]{:S(2)}) collective-permute-start(bf16[256,768]{1,0:T(8,128)(2,1)S(1)} %get-tuple-element.49), channel_id=1, source_target_pairs={{0,7},{1,4},{2,5},{3,6},{4,3},{5,0},{6,1},{7,2},{8,15},{9,12},{10,... | collective-permute-start | bytes 1179656 | tf_op jit(solution)/shard_map/ppermute | solution.py:396
  103.8 0.8 collective-permute-done.24
  104.6 3.5 %collective-permute-start.26 = (bf16[256,768]{1,0:T(8,128)(2,1)S(1)}, bf16[256,768]{1,0:T(8,128)(2,1)S(1)}, u32[]{:S(2)}, u32[]{:S(2)}) collective-permute-start(bf16[256,768]{1,0:T(8,128)(2,1)S(1)} %get-tuple-element.50), channel_id=1, source_target_pairs={{0,2},{1,3},{2,0},{3,1},{4,6},{5,7},{6,4},{7,5},{8,10},{9,11},{10,... | collective-permute-start | bytes 1179656 | tf_op jit(solution)/shard_map/ppermute | solution.py:396
  108.2 2.7 %collective-permute-done.19.c = bf16[2,144,768]{2,1,0:T(8,128)(2,1)S(1)} collective-permute-done((bf16[2,144,768]{2,1,0:T(8,128)(2,1)S(1)}, bf16[2,144,768]{2,1,0:T(8,128)(2,1)S(1)}, u32[]{:S(2)}, u32[]{:S(2)}) %collective-permute-start.19) | collective-permute-done | bytes 442400 | tf_op jit(solution)/shard_map/ppermute | solution.py:50
  110.9 2.6 %collective-permute-start.28 = (bf16[256,768]{1,0:T(8,128)(2,1)S(1)}, bf16[256,768]{1,0:T(8,128)(2,1)S(1)}, u32[]{:S(2)}, u32[]{:S(2)}) collective-permute-start(bf16[256,768]{1,0:T(8,128)(2,1)S(1)} %get-tuple-element.52), channel_id=1, source_target_pairs={{0,3},{1,0},{2,1},{3,2},{4,7},{5,4},{6,5},{7,6},{8,11},{9,8},{10,9... | collective-permute-start | bytes 1179656 | tf_op jit(solution)/shard_map/ppermute | solution.py:396
  113.6 3.2 %collective-permute-start.29 = (bf16[256,768]{1,0:T(8,128)(2,1)S(1)}, bf16[256,768]{1,0:T(8,128)(2,1)S(1)}, u32[]{:S(2)}, u32[]{:S(2)}) collective-permute-start(bf16[256,768]{1,0:T(8,128)(2,1)S(1)} %get-tuple-element.53), channel_id=1, source_target_pairs={{0,4},{1,5},{2,6},{3,7},{4,0},{5,1},{6,2},{7,3},{8,12},{9,13},{10,... | collective-permute-start | bytes 1179656 | tf_op jit(solution)/shard_map/ppermute | solution.py:396
  116.8 0.1 pair.4.a
  116.9 0.1 across.1
  117.0 1.9 %collective-permute-done.25 = bf16[256,768]{1,0:T(8,128)(2,1)S(1)} collective-permute-done((bf16[256,768]{1,0:T(8,128)(2,1)S(1)}, bf16[256,768]{1,0:T(8,128)(2,1)S(1)}, u32[]{:S(2)}, u32[]{:S(2)}) %collective-permute-start.25) | collective-permute-done | bytes 393248 | tf_op jit(solution)/shard_map/ppermute | solution.py:396
  118.9 6.6 %collective-permute-done.27 = bf16[256,768]{1,0:T(8,128)(2,1)S(1)} collective-permute-done((bf16[256,768]{1,0:T(8,128)(2,1)S(1)}, bf16[256,768]{1,0:T(8,128)(2,1)S(1)}, u32[]{:S(2)}, u32[]{:S(2)}) %collective-permute-start.27) | collective-permute-done | bytes 393248 | tf_op jit(solution)/shard_map/ppermute | solution.py:396
  125.5 3.7 %collective-permute-done.28 = bf16[256,768]{1,0:T(8,128)(2,1)S(1)} collective-permute-done((bf16[256,768]{1,0:T(8,128)(2,1)S(1)}, bf16[256,768]{1,0:T(8,128)(2,1)S(1)}, u32[]{:S(2)}, u32[]{:S(2)}) %collective-permute-start.28) | collective-permute-done | bytes 393248 | tf_op jit(solution)/shard_map/ppermute | solution.py:396
  129.2 1.2 add_convert_fusion
  130.4 0.8 finish.1
  131.2 0.8 slice.25
  131.9 1.2 slice.24
  133.1 0.1 add.154.radii_ref
  133.2 0.9 copy-done.1
  134.2 0.9 copy-done.3
  135.1 5.2 %bounds.1 = f32[1,2048]{1,0:T(1,128)} custom-call(s32[1]{0:T(128)} %bitcast.me_ref, bf16[512,768]{1,0:T(8,128)(2,1)S(1)} %bitcast.26, f32[1,512]{1,0:T(1,128)S(1)} %add.154.radii_ref, bf16[128,768]{1,0:T(8,128)(2,1)S(1)} %fusion.8.refs_0_.q0.refs_4_, bf16[128,768]{1,0:T(8,128)(2,1)S(1)} %collective-permute-done.refs_1_.q1.refs_5_, ...), custom_call_target="tpu_custom_call" | custom-call | flops 3200000000 | bytes 400000 | tf_op jit(solution)/shard_map/bounds/pallas_call | solution.py:332
  (53 shorter events, 0.2 us)
Async XLA Ops:
  7.2 124.0 %all-gather.3.cloned.1.call-start = ((), (), s32[]{:S(2)}) async-start(), calls=%async_computation | async-start | bytes 1253376 | tf_op jit(solution)/shard_map/all_gather | solution.py:366
  8.3 11.6 %copy-start.12 = (f32[32]{0:T(128)S(1)}, f32[32]{0:T(128)}, u32[]{:S(2)}) copy-start(f32[32]{0:T(128)} %param.16) | copy-start | bytes 388
  8.3 11.6 %copy-start.11 = (bf16[32,768]{1,0:T(8,128)(2,1)S(1)}, bf16[32,768]{1,0:T(8,128)(2,1)}, u32[]{:S(2)}) copy-start(bf16[32,768]{1,0:T(8,128)(2,1)} %param.15) | copy-start | bytes 147460
  8.3 17.0 %copy-start.4 = (s32[2048,16]{0,1:T(8,128)S(1)}, s32[2048,16]{0,1:T(8,128)}, u32[]{:S(2)}) copy-start(s32[2048,16]{0,1:T(8,128)} %param.17) | copy-start | bytes 393220
  8.3 17.0 %copy-start.5 = (s32[2048,4]{0,1:T(4,128)S(1)}, s32[2048,4]{0,1:T(4,128)}, u32[]{:S(2)}) copy-start(s32[2048,4]{0,1:T(4,128)} %param.18) | copy-start | bytes 98308
  8.3 17.0 %copy-start.6 = (s32[512]{0:T(512)S(1)}, s32[512]{0:T(512)}, u32[]{:S(2)}) copy-start(s32[512]{0:T(512)} %param.19) | copy-start | bytes 6148
  14.1 13.6 %collective-permute-start.11 = (bf16[128,768]{1,0:T(8,128)(2,1)S(1)}, bf16[128,768]{1,0:T(8,128)(2,1)S(1)}, u32[]{:S(2)}, u32[]{:S(2)}) collective-permute-start(bf16[128,768]{1,0:T(8,128)(2,1)S(1)} %fusion.8.refs_0_.q0.refs_4_), channel_id=1, source_target_pairs={{0,96},{8,104},{16,112},{24,120},{32,0},{40,8},{48,16},{56,24},{64... | collective-permute-start | bytes 589832 | tf_op jit(solution)/shard_map/ppermute | solution.py:50
  18.3 9.4 %collective-permute-start.7 = (bf16[128,768]{1,0:T(8,128)(2,1)S(1)}, bf16[128,768]{1,0:T(8,128)(2,1)S(1)}, u32[]{:S(2)}, u32[]{:S(2)}) collective-permute-start(bf16[128,768]{1,0:T(8,128)(2,1)S(1)} %fusion.8.refs_0_.q0.refs_4_), channel_id=1, source_target_pairs={{0,64},{8,72},{16,80},{24,88},{32,96},{40,104},{48,112},{56,120},{... | collective-permute-start | bytes 589832 | tf_op jit(solution)/shard_map/ppermute | solution.py:50
  18.3 6.4 %collective-permute-start.1 = (bf16[128,768]{1,0:T(8,128)(2,1)S(1)}, bf16[128,768]{1,0:T(8,128)(2,1)S(1)}, u32[]{:S(2)}, u32[]{:S(2)}) collective-permute-start(bf16[128,768]{1,0:T(8,128)(2,1)S(1)} %fusion.8.refs_0_.q0.refs_4_), channel_id=1, source_target_pairs={{0,16},{8,24},{16,0},{24,8},{32,48},{40,56},{48,32},{56,40},{64,80... | collective-permute-start | bytes 589832 | tf_op jit(solution)/shard_map/ppermute | solution.py:50
  19.8 13.0 %collective-permute-start = (bf16[128,768]{1,0:T(8,128)(2,1)S(1)}, bf16[128,768]{1,0:T(8,128)(2,1)S(1)}, u32[]{:S(2)}, u32[]{:S(2)}) collective-permute-start(bf16[128,768]{1,0:T(8,128)(2,1)S(1)} %fusion.8.refs_0_.q0.refs_4_), channel_id=1, source_target_pairs={{0,8},{8,0},{16,24},{24,16},{32,40},{40,32},{48,56},{56,48},{64,72... | collective-permute-start | bytes 589832 | tf_op jit(solution)/shard_map/ppermute | solution.py:50
  24.6 8.4 %collective-permute-start.13 = (bf16[128,768]{1,0:T(8,128)(2,1)S(1)}, bf16[128,768]{1,0:T(8,128)(2,1)S(1)}, u32[]{:S(2)}, u32[]{:S(2)}) collective-permute-start(bf16[128,768]{1,0:T(8,128)(2,1)S(1)} %collective-permute-done.1.refs_2_.q2.refs_6_), channel_id=1, source_target_pairs={{0,96},{8,104},{16,112},{24,120},{32,0},{40,8},{48,16},{56,24},{64... | collective-permute-start | bytes 589832 | tf_op jit(solution)/shard_map/ppermute | solution.py:50
  25.3 7.7 %collective-permute-start.2 = (bf16[128,768]{1,0:T(8,128)(2,1)S(1)}, bf16[128,768]{1,0:T(8,128)(2,1)S(1)}, u32[]{:S(2)}, u32[]{:S(2)}) collective-permute-start(bf16[128,768]{1,0:T(8,128)(2,1)S(1)} %collective-permute-done.1.refs_2_.q2.refs_6_), channel_id=1, source_target_pairs={{0,8},{8,0},{16,24},{24,16},{32,40},{40,32},{48,56},{56,48},{64,72... | collective-permute-start | bytes 589832 | tf_op jit(solution)/shard_map/ppermute | solution.py:50
  27.7 15.1 %collective-permute-start.3 = (bf16[128,768]{1,0:T(8,128)(2,1)S(1)}, bf16[128,768]{1,0:T(8,128)(2,1)S(1)}, u32[]{:S(2)}, u32[]{:S(2)}) collective-permute-start(bf16[128,768]{1,0:T(8,128)(2,1)S(1)} %fusion.8.refs_0_.q0.refs_4_), channel_id=1, source_target_pairs={{0,32},{8,40},{16,48},{24,56},{32,64},{40,72},{48,80},{56,88},{64,... | collective-permute-start | bytes 589832 | tf_op jit(solution)/shard_map/ppermute | solution.py:50
  27.7 16.5 %collective-permute-start.9 = (bf16[128,768]{1,0:T(8,128)(2,1)S(1)}, bf16[128,768]{1,0:T(8,128)(2,1)S(1)}, u32[]{:S(2)}, u32[]{:S(2)}) collective-permute-start(bf16[128,768]{1,0:T(8,128)(2,1)S(1)} %collective-permute-done.1.refs_2_.q2.refs_6_), channel_id=1, source_target_pairs={{0,64},{8,72},{16,80},{24,88},{32,96},{40,104},{48,112},{56,120},{... | collective-permute-start | bytes 589832 | tf_op jit(solution)/shard_map/ppermute | solution.py:50
  32.9 11.3 %collective-permute-start.5 = (bf16[128,768]{1,0:T(8,128)(2,1)S(1)}, bf16[128,768]{1,0:T(8,128)(2,1)S(1)}, u32[]{:S(2)}, u32[]{:S(2)}) collective-permute-start(bf16[128,768]{1,0:T(8,128)(2,1)S(1)} %collective-permute-done.1.refs_2_.q2.refs_6_), channel_id=1, source_target_pairs={{0,32},{8,40},{16,48},{24,56},{32,64},{40,72},{48,80},{56,88},{64,... | collective-permute-start | bytes 589832 | tf_op jit(solution)/shard_map/ppermute | solution.py:50
  33.0 9.9 %collective-permute-start.12 = (bf16[128,768]{1,0:T(8,128)(2,1)S(1)}, bf16[128,768]{1,0:T(8,128)(2,1)S(1)}, u32[]{:S(2)}, u32[]{:S(2)}) collective-permute-start(bf16[128,768]{1,0:T(8,128)(2,1)S(1)} %collective-permute-done.11.refs_12_.q0.refs_16_), channel_id=1, source_target_pairs={{0,8},{8,0},{16,24},{24,16},{32,40},{40,32},{48,56},{56,48},{64,72... | collective-permute-start | bytes 589832 | tf_op jit(solution)/shard_map/ppermute | solution.py:50
  33.0 11.7 %collective-permute-start.14 = (bf16[128,768]{1,0:T(8,128)(2,1)S(1)}, bf16[128,768]{1,0:T(8,128)(2,1)S(1)}, u32[]{:S(2)}, u32[]{:S(2)}) collective-permute-start(bf16[128,768]{1,0:T(8,128)(2,1)S(1)} %collective-permute-done.13.refs_14_.q2.refs_18_), channel_id=1, source_target_pairs={{0,8},{8,0},{16,24},{24,16},{32,40},{40,32},{48,56},{56,48},{64,72... | collective-permute-start | bytes 589832 | tf_op jit(solution)/shard_map/ppermute | solution.py:50
  41.4 1.3 copy-start.7
  42.8 11.3 %collective-permute-start.8 = (bf16[128,768]{1,0:T(8,128)(2,1)S(1)}, bf16[128,768]{1,0:T(8,128)(2,1)S(1)}, u32[]{:S(2)}, u32[]{:S(2)}) collective-permute-start(bf16[128,768]{1,0:T(8,128)(2,1)S(1)} %collective-permute-done.7.refs_8_.q0.refs_12_), channel_id=1, source_target_pairs={{0,8},{8,0},{16,24},{24,16},{32,40},{40,32},{48,56},{56,48},{64,72... | collective-permute-start | bytes 589832 | tf_op jit(solution)/shard_map/ppermute | solution.py:50
  42.8 21.1 %collective-permute-start.4 = (bf16[128,768]{1,0:T(8,128)(2,1)S(1)}, bf16[128,768]{1,0:T(8,128)(2,1)S(1)}, u32[]{:S(2)}, u32[]{:S(2)}) collective-permute-start(bf16[128,768]{1,0:T(8,128)(2,1)S(1)} %collective-permute-done.3.refs_4_.q0.refs_8_), channel_id=1, source_target_pairs={{0,8},{8,0},{16,24},{24,16},{32,40},{40,32},{48,56},{56,48},{64,72... | collective-permute-start | bytes 589832 | tf_op jit(solution)/shard_map/ppermute | solution.py:50
  44.2 47.6 %collective-permute-start.15 = (bf16[2,144,768]{2,1,0:T(8,128)(2,1)S(1)}, bf16[2,144,768]{2,1,0:T(8,128)(2,1)S(1)}, u32[]{:S(2)}, u32[]{:S(2)}) collective-permute-start(bf16[2,144,768]{2,1,0:T(8,128)(2,1)S(1)} %get-tuple-element.33), channel_id=1, source_target_pairs={{0,8},{8,0},{16,24},{24,16},{32,40},{40,32},{48,56},{56,48},{64,72... | collective-permute-start | bytes 1327112 | tf_op jit(solution)/shard_map/ppermute | solution.py:50
  44.2 10.3 %collective-permute-start.10 = (bf16[128,768]{1,0:T(8,128)(2,1)S(1)}, bf16[128,768]{1,0:T(8,128)(2,1)S(1)}, u32[]{:S(2)}, u32[]{:S(2)}) collective-permute-start(bf16[128,768]{1,0:T(8,128)(2,1)S(1)} %collective-permute-done.9.refs_10_.q2.refs_14_), channel_id=1, source_target_pairs={{0,8},{8,0},{16,24},{24,16},{32,40},{40,32},{48,56},{56,48},{64,72... | collective-permute-start | bytes 589832 | tf_op jit(solution)/shard_map/ppermute | solution.py:50
  44.7 19.3 %collective-permute-start.6 = (bf16[128,768]{1,0:T(8,128)(2,1)S(1)}, bf16[128,768]{1,0:T(8,128)(2,1)S(1)}, u32[]{:S(2)}, u32[]{:S(2)}) collective-permute-start(bf16[128,768]{1,0:T(8,128)(2,1)S(1)} %collective-permute-done.5.refs_6_.q2.refs_10_), channel_id=1, source_target_pairs={{0,8},{8,0},{16,24},{24,16},{32,40},{40,32},{48,56},{56,48},{64,72... | collective-permute-start | bytes 589832 | tf_op jit(solution)/shard_map/ppermute | solution.py:50
  52.7 1.3 copy-start.8
  54.0 31.8 %collective-permute-start.20 = (bf16[2,144,768]{2,1,0:T(8,128)(2,1)S(1)}, bf16[2,144,768]{2,1,0:T(8,128)(2,1)S(1)}, u32[]{:S(2)}, u32[]{:S(2)}) collective-permute-start(bf16[2,144,768]{2,1,0:T(8,128)(2,1)S(1)} %get-tuple-element.39), channel_id=1, source_target_pairs={{0,8},{8,0},{16,24},{24,16},{32,40},{40,32},{48,56},{56,48},{64,72... | collective-permute-start | bytes 1327112 | tf_op jit(solution)/shard_map/ppermute | solution.py:50
  54.5 37.6 %copy-start = (bf16[128,768]{1,0:T(8,128)(2,1)}, bf16[128,768]{1,0:T(8,128)(2,1)S(1)}, u32[]{:S(2)}) copy-start(bf16[128,768]{1,0:T(8,128)(2,1)S(1)} %collective-permute-done.10.refs_11_.q3.refs_15_) | copy-start | bytes 589828
  62.5 1.4 copy-start.9
  63.9 22.5 %collective-permute-start.18 = (bf16[2,144,768]{2,1,0:T(8,128)(2,1)S(1)}, bf16[2,144,768]{2,1,0:T(8,128)(2,1)S(1)}, u32[]{:S(2)}, u32[]{:S(2)}) collective-permute-start(bf16[2,144,768]{2,1,0:T(8,128)(2,1)S(1)} %get-tuple-element.37), channel_id=1, source_target_pairs={{0,8},{8,0},{16,24},{24,16},{32,40},{40,32},{48,56},{56,48},{64,72... | collective-permute-start | bytes 1327112 | tf_op jit(solution)/shard_map/ppermute | solution.py:50
  63.9 28.1 %copy-start.2 = (bf16[128,768]{1,0:T(8,128)(2,1)}, bf16[128,768]{1,0:T(8,128)(2,1)S(1)}, u32[]{:S(2)}) copy-start(bf16[128,768]{1,0:T(8,128)(2,1)S(1)} %collective-permute-done.6.refs_7_.q3.refs_11_) | copy-start | bytes 589828
  72.0 1.4 copy-start.10
  73.4 14.6 %collective-permute-start.16 = (bf16[2,144,768]{2,1,0:T(8,128)(2,1)S(1)}, bf16[2,144,768]{2,1,0:T(8,128)(2,1)S(1)}, u32[]{:S(2)}, u32[]{:S(2)}) collective-permute-start(bf16[2,144,768]{2,1,0:T(8,128)(2,1)S(1)} %get-tuple-element.35), channel_id=1, source_target_pairs={{0,8},{8,0},{16,24},{24,16},{32,40},{40,32},{48,56},{56,48},{64,72... | collective-permute-start | bytes 1327112 | tf_op jit(solution)/shard_map/ppermute | solution.py:50
  80.2 18.3 %collective-permute-start.23 = (bf16[256,768]{1,0:T(8,128)(2,1)S(1)}, bf16[256,768]{1,0:T(8,128)(2,1)S(1)}, u32[]{:S(2)}, u32[]{:S(2)}) collective-permute-start(bf16[256,768]{1,0:T(8,128)(2,1)S(1)} %get-tuple-element.47), channel_id=1, source_target_pairs={{0,6},{1,7},{2,4},{3,5},{4,2},{5,3},{6,0},{7,1},{8,14},{9,15},{10,... | collective-permute-start | bytes 1179656 | tf_op jit(solution)/shard_map/ppermute | solution.py:396
  85.9 18.8 %collective-permute-start.24 = (bf16[256,768]{1,0:T(8,128)(2,1)S(1)}, bf16[256,768]{1,0:T(8,128)(2,1)S(1)}, u32[]{:S(2)}, u32[]{:S(2)}) collective-permute-start(bf16[256,768]{1,0:T(8,128)(2,1)S(1)} %get-tuple-element.48), channel_id=1, source_target_pairs={{0,5},{1,6},{2,7},{3,4},{4,1},{5,2},{6,3},{7,0},{8,13},{9,14},{10,... | collective-permute-start | bytes 1179656 | tf_op jit(solution)/shard_map/ppermute | solution.py:396
  86.3 21.8 %collective-permute-start.21 = (bf16[2,144,768]{2,1,0:T(8,128)(2,1)S(1)}, bf16[2,144,768]{2,1,0:T(8,128)(2,1)S(1)}, u32[]{:S(2)}, u32[]{:S(2)}) collective-permute-start(bf16[2,144,768]{2,1,0:T(8,128)(2,1)S(1)} %pair.7), channel_id=1, source_target_pairs={{0,32},{8,40},{16,48},{24,56},{32,64},{40,72},{48,80},{56,88},{64,... | collective-permute-start | bytes 1327112 | tf_op jit(solution)/shard_map/ppermute | solution.py:50
  88.0 22.9 %collective-permute-start.19 = (bf16[2,144,768]{2,1,0:T(8,128)(2,1)S(1)}, bf16[2,144,768]{2,1,0:T(8,128)(2,1)S(1)}, u32[]{:S(2)}, u32[]{:S(2)}) collective-permute-start(bf16[2,144,768]{2,1,0:T(8,128)(2,1)S(1)} %pair.6), channel_id=1, source_target_pairs={{0,64},{8,72},{16,80},{24,88},{32,96},{40,104},{48,112},{56,120},{... | collective-permute-start | bytes 1327112 | tf_op jit(solution)/shard_map/ppermute | solution.py:50
  91.8 21.8 %collective-permute-start.17 = (bf16[2,144,768]{2,1,0:T(8,128)(2,1)S(1)}, bf16[2,144,768]{2,1,0:T(8,128)(2,1)S(1)}, u32[]{:S(2)}, u32[]{:S(2)}) collective-permute-start(bf16[2,144,768]{2,1,0:T(8,128)(2,1)S(1)} %pair.5), channel_id=1, source_target_pairs={{0,96},{8,104},{16,112},{24,120},{32,0},{40,8},{48,16},{56,24},{64... | collective-permute-start | bytes 1327112 | tf_op jit(solution)/shard_map/ppermute | solution.py:50
  98.5 20.4 %collective-permute-start.25 = (bf16[256,768]{1,0:T(8,128)(2,1)S(1)}, bf16[256,768]{1,0:T(8,128)(2,1)S(1)}, u32[]{:S(2)}, u32[]{:S(2)}) collective-permute-start(bf16[256,768]{1,0:T(8,128)(2,1)S(1)} %get-tuple-element.49), channel_id=1, source_target_pairs={{0,7},{1,4},{2,5},{3,6},{4,3},{5,0},{6,1},{7,2},{8,15},{9,12},{10,... | collective-permute-start | bytes 1179656 | tf_op jit(solution)/shard_map/ppermute | solution.py:396
  104.6 14.3 %collective-permute-start.26 = (bf16[256,768]{1,0:T(8,128)(2,1)S(1)}, bf16[256,768]{1,0:T(8,128)(2,1)S(1)}, u32[]{:S(2)}, u32[]{:S(2)}) collective-permute-start(bf16[256,768]{1,0:T(8,128)(2,1)S(1)} %get-tuple-element.50), channel_id=1, source_target_pairs={{0,2},{1,3},{2,0},{3,1},{4,6},{5,7},{6,4},{7,5},{8,10},{9,11},{10,... | collective-permute-start | bytes 1179656 | tf_op jit(solution)/shard_map/ppermute | solution.py:396
  108.2 17.3 %collective-permute-start.27 = (bf16[256,768]{1,0:T(8,128)(2,1)S(1)}, bf16[256,768]{1,0:T(8,128)(2,1)S(1)}, u32[]{:S(2)}, u32[]{:S(2)}) collective-permute-start(bf16[256,768]{1,0:T(8,128)(2,1)S(1)} %get-tuple-element.51), channel_id=1, source_target_pairs={{0,1},{1,2},{2,3},{3,0},{4,5},{5,6},{6,7},{7,4},{8,9},{9,10},{10,1... | collective-permute-start | bytes 1179656 | tf_op jit(solution)/shard_map/ppermute | solution.py:396
  110.9 18.2 %collective-permute-start.28 = (bf16[256,768]{1,0:T(8,128)(2,1)S(1)}, bf16[256,768]{1,0:T(8,128)(2,1)S(1)}, u32[]{:S(2)}, u32[]{:S(2)}) collective-permute-start(bf16[256,768]{1,0:T(8,128)(2,1)S(1)} %get-tuple-element.52), channel_id=1, source_target_pairs={{0,3},{1,0},{2,1},{3,2},{4,7},{5,4},{6,5},{7,6},{8,11},{9,8},{10,9... | collective-permute-start | bytes 1179656 | tf_op jit(solution)/shard_map/ppermute | solution.py:396
  113.6 15.6 %collective-permute-start.29 = (bf16[256,768]{1,0:T(8,128)(2,1)S(1)}, bf16[256,768]{1,0:T(8,128)(2,1)S(1)}, u32[]{:S(2)}, u32[]{:S(2)}) collective-permute-start(bf16[256,768]{1,0:T(8,128)(2,1)S(1)} %get-tuple-element.53), channel_id=1, source_target_pairs={{0,4},{1,5},{2,6},{3,7},{4,0},{5,1},{6,2},{7,3},{8,12},{9,13},{10,... | collective-permute-start | bytes 1179656 | tf_op jit(solution)/shard_map/ppermute | solution.py:396
  118.9 11.5 %collective-permute-start.22 = (bf16[144,768]{1,0:T(8,128)(2,1)S(1)}, bf16[144,768]{1,0:T(8,128)(2,1)S(1)}, u32[]{:S(2)}, u32[]{:S(2)}) collective-permute-start(bf16[144,768]{1,0:T(8,128)(2,1)S(1)} %across.1), channel_id=1, source_target_pairs={{0,16},{8,24},{16,0},{24,8},{32,48},{40,56},{48,32},{56,40},{64,80... | collective-permute-start | bytes 663560 | tf_op jit(solution)/shard_map/ppermute | solution.py:50
  133.2 0.9 copy-start.1
  134.2 0.9 copy-start.3
Sparse Core Ops, SparseCore 0:
  20.7 37.7 all-gather.2

commit v2 on v0

v2 whole, which is shorter than its diff:
```python
import functools

import jax
import jax.numpy as jnp
from jax import lax
from jax.experimental import pallas as pl
from jax.experimental.pallas import tpu as pltpu
from jax.sharding import PartitionSpec as P

F32 = jnp.float32
BF16 = jnp.bfloat16

NZ, NY = 4, 2
NX, NYH = 4, 2
ROWS = 128
PAIR = 2 * ROWS
PAIRS = 8
EXTRA = 16
D = 768
FF = 3072
FTILE = 1024
BL = 64
K = 16
P_SIZE = 4
LBLK = 32
LOCAL = LBLK * BL
BLOCKS = 512
TILE = 256
CROWS = 48
LN2 = 0.6931471805599453
MIB = 1024 * 1024

SOURCE = (
    ((0, 0), (0, 0)),
    ((-1, 0), (1, 0)),
    ((1, 0), (-1, 0)),
    ((0, 1), (2, 0)),
    ((2, 0), (0, 1)),
    ((-1, 1), (1, 1)),
    ((1, 1), (-1, 1)),
    ((2, 1), (2, 1)),
)

DP_ORDER = ((2, 1), (1, 1), (3, 1), (2, 0), (1, 0), (3, 0), (0, 1), (0, 0))


def send_label(x, steps, core=0):
    at = lambda z, y, c: (z % NZ) * 4 + (y % NY) * 2 + c % 2
    perm = [
        (at(z, y, c), at(z + steps[c][0], y + steps[c][1], c + core))
        for z in range(NZ)
        for y in range(NY)
        for c in range(2)
    ]
    return lax.ppermute(x, "label", perm)


def swap(x):
    return send_label(x, SOURCE[0], 1)


def to_source(x, p):
    return send_label(x, SOURCE[p])


def from_source(x, p):
    return send_label(x, [(-z, -y) for z, y in SOURCE[p]])


def dp_perm(dx, dy):
    at = lambda x, y: (y % NYH) * 4 + x % NX
    return [(at(x, y), at(x + dx, y + dy)) for y in range(NYH) for x in range(NX)]


VMEM = pl.BlockSpec(memory_space=pltpu.VMEM)
SMEM = pl.BlockSpec(memory_space=pltpu.SMEM)


def call(kernel, name, us, out, specs, args, scratch=(), limit=20):
    return pl.pallas_call(
        kernel,
        out_shape=out,
        in_specs=specs,
        out_specs=jax.tree.map(lambda _: VMEM, out),
        scratch_shapes=list(scratch),
        compiler_params=pltpu.CompilerParams(vmem_limit_bytes=limit * MIB),
        cost_estimate=pl.CostEstimate(
            flops=int(us * 8e8), bytes_accessed=int(us * 1e5), transcendentals=0
        ),
        name=name,
    )(*args)


def array(*shape, dtype=BF16):
    return jax.ShapeDtypeStruct(shape, dtype)


def first_query(me, p, b):
    z, y, c = me // 4, (me // 2) % 2, me % 2
    (z0, y0), (z1, y1) = SOURCE[p]
    z = lax.rem(z + NZ + z0 + c * (z1 - z0), NZ)
    y = lax.rem(y + NY + y0 + c * (y1 - y0), NY)
    return pl.multiple_of((z * 4 + y * 2 + b) * ROWS, ROWS)


def encode_kernel(x_ref, gain_ref, w_in_ref, w_out_ref, out_ref, normed_ref, total_ref):
    i = pl.program_id(0)

    @pl.when(i == 0)
    def _():
        values = x_ref[...].astype(F32)
        meansq = jnp.mean(values * values, axis=-1, keepdims=True)
        normed_ref[...] = (values * lax.rsqrt(meansq + 1e-06) * gain_ref[...]).astype(BF16)
        total_ref[...] = values

    active = jax.nn.gelu(
        jnp.dot(normed_ref[...], w_in_ref[...], preferred_element_type=F32), approximate=True
    ).astype(BF16)
    total_ref[...] += jnp.dot(active, w_out_ref[...], preferred_element_type=F32)

    @pl.when(i == pl.num_programs(0) - 1)
    def _():
        out_ref[...] = total_ref[...].astype(BF16)


def encode(hidden_in, norm_gain, w_in, w_out):
    whole = lambda *shape: pl.BlockSpec(shape, lambda i: (0, 0))
    return pl.pallas_call(
        encode_kernel,
        out_shape=array(ROWS, D),
        grid=(FF // FTILE,),
        in_specs=[
            whole(ROWS, D),
            whole(1, D),
            pl.BlockSpec((D, FTILE), lambda i: (0, i)),
            pl.BlockSpec((FTILE, D), lambda i: (i, 0)),
        ],
        out_specs=whole(ROWS, D),
        scratch_shapes=[pltpu.VMEM((ROWS, D), BF16), pltpu.VMEM((ROWS, D), F32)],
        compiler_params=pltpu.CompilerParams(vmem_limit_bytes=24 * MIB),
        cost_estimate=pl.CostEstimate(
            flops=int(4e9), bytes_accessed=int(1e7), transcendentals=0
        ),
        name="encode",
    )(hidden_in, norm_gain.reshape(1, D), w_in, w_out)


def join_kernel(me_ref, own_ref, other_ref, out_ref):
    c = me_ref[0] % 2
    out_ref[pl.ds(pl.multiple_of(c * ROWS, ROWS), ROWS), :] = own_ref[...]
    out_ref[pl.ds(pl.multiple_of((1 - c) * ROWS, ROWS), ROWS), :] = other_ref[...]


def join(me, own, other):
    return call(
        join_kernel, "join", 0.5, array(PAIR, D), [SMEM, VMEM, VMEM], (me, own, other)
    )


def prepare_kernel(me_ref, sl_ref, pos_ref, bs_ref, *refs):
    half_refs, count_refs = refs[:PAIRS], refs[PAIRS : 2 * PAIRS]
    base_ref, wa_ref, wb_ref = refs[2 * PAIRS :]
    me = me_ref[0]
    slot_rows = lax.broadcasted_iota(jnp.int32, (LBLK, BLOCKS), 0) + me * LBLK
    ids = lax.broadcasted_iota(jnp.int32, (LBLK, BLOCKS), 1).astype(F32)
    here = jnp.sum(jnp.where(bs_ref[...] == slot_rows, ids, 0.0), axis=1, keepdims=True)
    here = jnp.broadcast_to(here, (LBLK, ROWS))
    which = lax.broadcasted_iota(jnp.int32, (K, ROWS), 0)
    shift = lax.broadcasted_iota(jnp.int32, (32, PAIR), 0)
    for p in range(PAIRS):
        for b in range(2):
            lanes = pl.ds(first_query(me, p, b), ROWS)
            sl = sl_ref[:, lanes].astype(F32)
            pos = pos_ref[:, lanes]
            base = jnp.zeros((LBLK, ROWS), F32)
            for k in range(K):
                base = jnp.where(here == sl[k : k + 1], 0.5, base)
            wa = jnp.zeros((LBLK, ROWS), jnp.int32)
            wb = jnp.zeros((LBLK, ROWS), jnp.int32)
            for n in range(P_SIZE):
                kp, jp = pos[n : n + 1] >> 6, pos[n : n + 1] & 63
                bid = jnp.sum(jnp.where(which == kp, sl, 0.0), axis=0, keepdims=True)
                bit = jnp.full((1, ROWS), 1, jnp.int32) << (31 - (jp & 31))
                match = here == bid
                wa = wa | jnp.where(match, jnp.where(jp < 32, bit, 0), 0)
                wb = wb | jnp.where(match, jnp.where(jp < 32, 0, bit), 0)
            out = slice(b * ROWS, (b + 1) * ROWS)
            base_ref[:, out] = base
            wa_ref[:, out] = wa
            wb_ref[:, out] = wb
        count_refs[p][...] = 2.0 * jnp.sum(base_ref[...], axis=0, keepdims=True)
        half_ref = half_refs[p]

        def slot(s, carry):
            base = base_ref[pl.ds(s, 1), :]
            for n, w_ref in enumerate((wa_ref, wb_ref)):
                hit = (w_ref[pl.ds(s, 1), :] << shift) < 0
                rows = pl.ds(pl.multiple_of(s * BL + n * 32, 32), 32)
                half_ref[rows, :] = jnp.where(hit, -base, base).astype(BF16)
            return carry

        lax.fori_loop(0, LBLK, slot, 0, unroll=4)


def prepare(me, sl, pos, bs):
    out = [array(LOCAL, PAIR)] * PAIRS + [array(1, PAIR, dtype=F32)] * PAIRS
    scratch = [pltpu.VMEM((LBLK, PAIR), t) for t in (F32, jnp.int32, jnp.int32)]
    outs = call(
        prepare_kernel, "prepare", 4, out, [SMEM] + [VMEM] * 3, (me, sl, pos, bs), scratch
    )
    return outs[:PAIRS], outs[PAIRS:]


def slope_kernel(q_ref, c_ref, half_ref, count_ref, s_ref, loss_ref, x0_ref, x1_ref):
    x_refs = (x0_ref, x1_ref)
    steps = LOCAL // TILE

    def logits(i):
        x_refs[i % 2][...] = lax.dot_general(
            c_ref[i * TILE : (i + 1) * TILE, :],
            q_ref[...],
            (((1,), (1,)), ((), ())),
            preferred_element_type=F32,
        )

    logits(0)
    losses = [LN2 * BL / 8 * jnp.broadcast_to(count_ref[...], (8, PAIR))[:, t * ROWS : (t + 1) * ROWS]
              for t in range(2)]
    for i in range(steps):
        if i + 1 < steps:
            logits(i + 1)
        for t in range(2):
            lanes = slice(t * ROWS, (t + 1) * ROWS)
            prod = jnp.ones((8, ROWS), F32)
            relu = jnp.zeros((8, ROWS), F32)
            for n in range(TILE // BL):
                rows = slice(i * TILE + n * BL, i * TILE + (n + 1) * BL)
                half = half_ref[rows, lanes].astype(F32)
                y = x_refs[i % 2][n * BL : (n + 1) * BL, lanes] * half
                th = jnp.tanh(y)
                s_ref[rows, lanes] = (half * th + half).astype(BF16)
                u8 = (1.0 + jnp.abs(th)).reshape(BL // 8, 8, ROWS)
                r8 = jnp.maximum(y, 0.0).reshape(BL // 8, 8, ROWS)
                for m in range(BL // 8):
                    prod = prod * u8[m]
                    relu = relu + r8[m]
            losses[t] = losses[t] + (2.0 * relu - jnp.log(prod))
    loss_ref[...] = jnp.sum(jnp.concatenate(losses, axis=1), axis=0, keepdims=True)


def slopes(q, classifier, half, count):
    return call(
        slope_kernel,
        "slopes",
        1.5,
        (array(LOCAL, PAIR), array(1, PAIR, dtype=F32)),
        [VMEM] * 4,
        (q, classifier, half, count),
        [pltpu.VMEM((TILE, PAIR), F32)] * 2,
    )


def loss_rows(row):
    hi = row.astype(BF16)
    rest = row - hi.astype(F32)
    mid = rest.astype(BF16)
    lo = (rest - mid.astype(F32)).astype(BF16)
    return jnp.concatenate([hi, mid, lo, jnp.zeros((EXTRA, D - 3 * ROWS), BF16)], axis=1)


def joined(rows):
    return rows[:, :ROWS] + rows[:, ROWS : 2 * ROWS] + rows[:, 2 * ROWS : 3 * ROWS]


def query_partial(s_ref, c_ref):
    return lax.dot_general(
        s_ref[...], c_ref[...], (((0,), (0,)), ((), ())), preferred_element_type=F32
    )


def loss_block(loss_ref, b):
    return jnp.broadcast_to(loss_ref[:, b * ROWS : (b + 1) * ROWS], (EXTRA, ROWS))


def give_kernel(me_ref, c_ref, s2, s4, s6, s7, l2, l4, l6, l7, g2, g4, g6, keep7, give7, t_ref):
    for s_ref, l_ref, out in ((s2, l2, g2), (s4, l4, g4), (s6, l6, g6)):
        total = query_partial(s_ref, c_ref)
        for b in range(2):
            out[b, :ROWS, :] = total[b * ROWS : (b + 1) * ROWS].astype(BF16)
            out[b, ROWS:, :] = loss_rows(loss_block(l_ref, b))
    total = query_partial(s7, c_ref)
    for b in range(2):
        t_ref[b, :ROWS, :] = total[b * ROWS : (b + 1) * ROWS].astype(BF16)
        t_ref[b, ROWS:, :] = loss_rows(loss_block(l7, b))
    c = me_ref[0] % 2
    keep7[...] = t_ref[c]
    give7[...] = t_ref[1 - c]


def take_kernel(c_ref, s1, s3, s5, l1, l3, l5, r1, r3, r5, keep7, r7, o1, o3, o5, o7):
    for s_ref, l_ref, r_ref, out in ((s1, l1, r1, o1), (s3, l3, r3, o3), (s5, l5, r5, o5)):
        total = query_partial(s_ref, c_ref).astype(BF16).astype(F32)
        for b in range(2):
            out[b, :ROWS, :] = (
                total[b * ROWS : (b + 1) * ROWS] + r_ref[b, :ROWS, :].astype(F32)
            ).astype(BF16)
            out[b, ROWS:, :] = loss_rows(
                loss_block(l_ref, b) + joined(r_ref[b, ROWS:, :].astype(F32))
            )
    total = keep7[...].astype(F32) + r7[...].astype(F32)
    o7[:ROWS, :] = total[:ROWS].astype(BF16)
    o7[ROWS:, :] = loss_rows(joined(total[ROWS:]))


def own_kernel(c_ref, s_ref, l_ref, out_ref):
    total = query_partial(s_ref, c_ref)
    for b in range(2):
        out_ref[b, :ROWS, :] = total[b * ROWS : (b + 1) * ROWS].astype(BF16)
        out_ref[b, ROWS:, :] = loss_rows(loss_block(l_ref, b))


def collect_kernel(me_ref, own, a, b, d, keep, give):
    c = me_ref[0] % 2
    keep[...] = sum(r[c].astype(F32) for r in (own, a, b, d))
    total = sum(r[1 - c].astype(F32) for r in (own, a, b, d))
    give[:ROWS, :] = total[:ROWS].astype(BF16)
    give[ROWS:, :] = loss_rows(joined(total[ROWS:]))


def finish_kernel(keep, other, far, grad_ref, loss_ref):
    total = keep[...] + other[...].astype(F32) + far[...].astype(F32)
    grad_ref[...] = total[:ROWS].astype(BF16)
    loss_ref[...] = joined(total[ROWS : ROWS + 8])[:1]


def class_kernel(count, order_ref, *refs):
    s_refs, q_refs, outs = refs[:PAIRS], refs[PAIRS : 2 * PAIRS], refs[2 * PAIRS :]
    rows = LOCAL // (NX * NYH)
    for n in range(count):
        at = pl.ds(pl.multiple_of(order_ref[n] * rows, rows), rows)
        slope = jnp.concatenate([s[at, :] for s in s_refs], axis=1)
        query = jnp.concatenate([q[...] for q in q_refs], axis=0)
        outs[n][...] = jnp.dot(slope, query, preferred_element_type=F32).astype(BF16)


def class_blocks(order, slope_pairs, pairs):
    count = order.shape[0]
    return call(
        functools.partial(class_kernel, count),
        "class_blocks",
        3.5,
        [array(LOCAL // (NX * NYH), D)] * count,
        [SMEM] + [VMEM] * (2 * PAIRS),
        (order, *slope_pairs, *pairs),
    )


def bound_kernel(me_ref, every_ref, *refs):
    q_refs, out_ref, cent_ref, radii_ref = refs[:PAIRS], refs[PAIRS], refs[-2], refs[-1]
    me = me_ref[0]
    for n in range(BLOCKS // LBLK):
        cent_ref[n * LBLK : (n + 1) * LBLK, :] = every_ref[n, :LBLK, :]
    for n in range(BLOCKS // ROWS):
        terms = sum(every_ref[4 * n + m, LBLK:, :ROWS].astype(F32) for m in range(4))
        radii_ref[:, n * ROWS : (n + 1) * ROWS] = terms[0:1] + terms[1:2] + terms[2:3]
    for p, q in enumerate(q_refs):
        for b in range(2):
            rows = slice(b * ROWS, (b + 1) * ROWS)
            value = q[rows, :].astype(F32)
            norm = jnp.sqrt(jnp.sum(value * value, axis=1, keepdims=True))
            score = lax.dot_general(
                q[rows, :], cent_ref[...], (((1,), (1,)), ((), ())), preferred_element_type=F32
            )
            top = jnp.max(score + norm * radii_ref[...], axis=1, keepdims=True)
            out_ref[:, pl.ds(first_query(me, p, b), ROWS)] = jnp.broadcast_to(
                top, (ROWS, ROWS)
            ).T[:1]


def after(value, *others):
    return lax.optimization_barrier((value, others))[0]


def on_device(
    hidden_in,
    norm_gain,
    w_in,
    w_out,
    classifier,
    centroids,
    radii,
    shortlist,
    positives,
    block_slot,
):
    label = lax.axis_index("label")
    dp = lax.axis_index("dp")
    me = label.astype(jnp.int32).reshape(1)

    hi = lax.reduce_precision(radii, 8, 7)
    mid = lax.reduce_precision(radii - hi, 8, 7)
    lo = lax.reduce_precision(radii - hi - mid, 8, 7)
    terms = jnp.tile(jnp.stack([hi, mid, lo]).astype(BF16), (1, D // LBLK))
    terms = jnp.where(jnp.arange(D) // LBLK == label % 4, terms, 0)
    packed = jnp.concatenate([centroids, jnp.pad(terms, ((0, CROWS - LBLK - 3), (0, 0)))], axis=0)
    every = lax.all_gather(packed, "label", axis=0)

    encoded = encode(hidden_in, norm_gain, w_in, w_out)

    pairs = [None] * PAIRS
    far = from_source(encoded, 7)
    pairs[0] = join(me, encoded, swap(encoded))
    for p in (1, 3, 5):
        pairs[p] = from_source(pairs[0], p)
        pairs[p + 1] = swap(pairs[p])
    pairs[7] = join(me, far, swap(far))

    halves, counts = prepare(
        after(me, encoded), shortlist.T, positives.T, block_slot.reshape(1, -1)
    )
    slope_pairs, losses = [None] * PAIRS, [None] * PAIRS
    for p in range(PAIRS):
        slope_pairs[p], losses[p] = slopes(pairs[p], classifier, halves[p], counts[p])

    order = jnp.stack(
        [((dp // NX + dy) % NYH) * NX + (dp % NX + dx) % NX for dx, dy in DP_ORDER]
    ).astype(jnp.int32)
    blocks = class_blocks(order[:4], slope_pairs, pairs)
    blocks = blocks + class_blocks(after(order[4:], blocks[0]), slope_pairs, pairs)
    class_total = blocks[-1].astype(F32)
    for (dx, dy), block in zip(DP_ORDER[:-1], blocks):
        class_total = class_total + lax.ppermute(block, "dp", dp_perm(dx, dy)).astype(F32)

    part = array(2, ROWS + EXTRA, D)
    half_part = array(ROWS + EXTRA, D)
    s, l = slope_pairs, losses
    g2, g4, g6, keep7, give7 = call(
        give_kernel,
        "give",
        4.5,
        (part, part, part, half_part, half_part),
        [SMEM] + [VMEM] * 9,
        (after(me, blocks[-1]), classifier, s[2], s[4], s[6], s[7], l[2], l[4], l[6], l[7]),
        [pltpu.VMEM((2, ROWS + EXTRA, D), BF16)],
    )
    r1, r3, r5, r7 = swap(g2), swap(g4), swap(g6), swap(give7)
    bound_top = call(
        bound_kernel,
        "bounds",
        4,
        array(1, PAIRS * PAIR, dtype=F32),
        [SMEM] + [VMEM] * (PAIRS + 1),
        (after(me, give7), every, *pairs),
        [pltpu.VMEM((BLOCKS, D), BF16), pltpu.VMEM((1, BLOCKS), F32)],
    )
    o1, o3, o5, o7 = call(
        take_kernel,
        "take",
        4,
        (part, part, part, half_part),
        [VMEM] * 12,
        (classifier, s[1], s[3], s[5], l[1], l[3], l[5], r1, r3, r5, keep7, r7),
    )
    own = call(own_kernel, "own", 1.2, part, [VMEM] * 3, (classifier, s[0], l[0]))
    keep, give = call(
        collect_kernel,
        "collect",
        1,
        (array(ROWS + EXTRA, D, dtype=F32), half_part),
        [SMEM] + [VMEM] * 4,
        (me, own, to_source(o1, 1), to_source(o3, 3), to_source(o5, 5)),
    )
    query_grad, loss = call(
        finish_kernel,
        "finish",
        1,
        (array(ROWS, D), array(1, ROWS, dtype=F32)),
        [VMEM] * 3,
        (keep, swap(give), to_source(o7, 7)),
    )
    return (
        bound_top.reshape(-1),
        loss.reshape(-1),
        query_grad,
        class_total.astype(BF16),
    )


def solution(mesh):
    placed = (
        P(("dp", "label"), None),
        P(),
        P(),
        P(),
        P("label", None),
        P("label", None),
        P("label"),
        P("dp", None),
        P("dp", None),
        P(),
    )
    return jax.shard_map(
        on_device,
        mesh=mesh,
        in_specs=placed,
        out_specs=(P("dp"), P(("dp", "label")), P(("dp", "label"), None), P(("label", "dp"), None)),
        check_vma=False,
    )
```

time: 778 us -> 166 us (0.21)
  local copies, waits for them, and re-layouts: 567 us -> 22.2 us
  blocking collectives: 60.7 us -> 0 us
  starting transfers between devices: 0.12 us -> 57.8 us
  matrix products: 50.6 us -> 0 us
  Pallas kernels: 0 us -> 47.1 us
  waiting for transfers between devices: 59.3 us -> 22 us
  other arithmetic: 20.3 us -> 1.99 us
    gather x36 -> x0, local copies, waits for them, and re-layouts: 563 us -> none  [the longest x1 345 us: on_device(): slots = block_slot[shortlist].reshape(-1)]
    reduce_scatter x2 -> x0, waiting for transfers between devices: 59.2 us -> none  [the longest x1 59.2 us: on_device(): lax.psum_scatter(grads, 'label', scatter_dimension=0, tiled=True)]
    ppermute x0 -> x25, starting transfers between devices: none -> 57.7 us  [the longest x7 34.6 us: on_device(): lax.ppermute(block, 'dp', dp_perm(dx, dy)).astype(F32)]
    dot_general x9 -> x0, matrix products: 50.6 us -> none  [the longest x1 11.3 us: on_device(): jnp.einsum('mrq,qc->mrc', selector, queries, preferred_element_type=jnp.f...]
    pallas_call x0 -> x20, Pallas kernels: none -> 47.1 us  [the longest x19 43.7 us: call(): pl.pallas_call(kernel, out_shape=out, in_specs=specs, out_specs=jax.tree....]
    unnamed x1 -> x0, blocking collectives: 32.3 us -> none
    pmax x1 -> x0, blocking collectives: 28.4 us -> none  [on_device(): bound_top = lax.pmax(jnp.max(scores, axis=-1), 'label')]
    ppermute x0 -> x25, waiting for transfers between devices: none -> 22 us  [the longest x7 14.3 us: on_device(): lax.ppermute(block, 'dp', dp_perm(dx, dy)).astype(F32)]
  transfers between devices with their start and end apart: 3 -> 26, of which waited for: 1 -> 6; matrix products, arithmetic and copies ran while one was open for 79% -> 1% of each run, Pallas kernels for 0% -> 23%
where the time goes in v2:
time: 166 us
  starting transfers between devices  57.8 us (35%)
  Pallas kernels  47.1 us (28%)
  local copies, waits for them, and re-layouts  22.2 us (13%)
  waiting for transfers between devices  22 us (13%)
  between operations  14.5 us (9%)
  other arithmetic  1.99 us (1%)
    pallas_call x19, Pallas kernels, call(): pl.pallas_call(kernel, out_shape=out, in_specs=specs, out_specs=jax.tree....  43.7 us
    ppermute x7, starting transfers between devices, on_device(): lax.ppermute(block, 'dp', dp_perm(dx, dy)).astype(F32)  34.6 us
    ppermute x18, starting transfers between devices, send_label(): return lax.ppermute(x, 'label', perm)  23.1 us
    unnamed x88, local copies, waits for them, and re-layouts  21.4 us
    ppermute x7, waiting for transfers between devices, on_device(): lax.ppermute(block, 'dp', dp_perm(dx, dy)).astype(F32)  14.3 us
    ppermute x18, waiting for transfers between devices, send_label(): return lax.ppermute(x, 'label', perm)  7.69 us
    pallas_call x1, Pallas kernels, encode(): pl.pallas_call(encode_kernel, out_shape=array(ROWS, D), grid=(FF // FTILE...  3.42 us
  transfers between devices with their start and end apart: 26, of which 6 were waited for; matrix products, arithmetic and copies ran while one was open for 1% of the time, Pallas kernels for 23%

profile of v2, /device:TPU:0, one launch (start us, length us, event | category | flops | bytes accessed | tf_op | source)
XLA Modules:
  0.0 165.6 jit_solution(9891402057113499316)
XLA Ops:
  7.2 0.7 reshape.55.gain_ref
  7.9 2.3 %copy-done.35 = bf16[768,3072]{1,0:T(8,128)(2,1)S(1)} copy-done((bf16[768,3072]{1,0:T(8,128)(2,1)S(1)}, bf16[768,3072]{1,0:T(8,128)(2,1)}, u32[]{:S(2)}) %copy-start.35) | copy-done | bytes 4718616
  10.2 2.3 %copy-done.36 = bf16[3072,768]{1,0:T(8,128)(2,1)S(1)} copy-done((bf16[3072,768]{1,0:T(8,128)(2,1)S(1)}, bf16[3072,768]{1,0:T(8,128)(2,1)}, u32[]{:S(2)}) %copy-start.36) | copy-done | bytes 4718616
  12.6 0.9 copy-done.38
  13.5 3.4 %encode.1.own_ref = bf16[128,768]{1,0:T(8,128)(2,1)} custom-call(bf16[128,768]{1,0:T(8,128)(2,1)S(1)} %copy-done.38, f32[1,768]{1,0:T(1,128)S(1)} %reshape.55.gain_ref, bf16[768,3072]{1,0:T(8,128)(2,1)S(1)} %copy-done.35, bf16[3072,768]{1,0:T(8,128)(2,1)S(1)} %copy-done.36), custom_call_target="tpu_custom_call" | custom-call | flops 4000000000 | bytes 10000000 | tf_op jit(solution)/shard_map/encode/pallas_call | solution.py:128
  16.9 5.0 %collective-permute-start.7 = (bf16[128,768]{1,0:T(8,128)(2,1)}, bf16[128,768]{1,0:T(8,128)(2,1)}, u32[]{:S(2)}, u32[]{:S(2)}) collective-permute-start(bf16[128,768]{1,0:T(8,128)(2,1)} %encode.1.own_ref), channel_id=1, source_target_pairs={{0,80},{8,88},{16,64},{24,72},{32,112},{40,120},{48,96},{56,104},{... | collective-permute-start | bytes 589832 | tf_op jit(solution)/shard_map/ppermute | solution.py:55
  22.1 0.6 fusion.1
  22.7 1.0 join.2.q_ref.refs_8_.refs_0_
  23.7 1.0 collective-permute-start.5
  24.7 0.9 copy-done.39
  25.6 0.8 copy-done.40
  26.3 0.7 copy-done.41
  27.0 3.6 %prepare.1 = (bf16[2048,256]{1,0:T(8,128)(2,1)S(1)}, bf16[2048,256]{1,0:T(8,128)(2,1)S(1)}, bf16[2048,256]{1,0:T(8,128)(2,1)S(1)}, bf16[2048,256]{1,0:T(8,128)(2...) custom-call(s32[1]{0:T(128)} %bitcast.me_ref, ...), custom_call_target="tpu_custom_call" | custom-call | flops 3200000000 | bytes 400000 | tf_op jit(solution)/shard_map/prepare/pallas_call | solution.py:80
  30.6 1.0 copy-done.9
  31.6 1.0 copy-done.11
  32.6 1.0 copy-done.13
  33.6 1.0 copy-done.15
  34.6 1.0 copy-done.17
  35.6 1.1 copy-done.19
  36.6 1.0 copy-done.21
  37.7 1.0 copy-done.23
  38.7 0.6 copy-done.25
  39.2 0.5 copy-done.27
  40.3 0.6 copy-done.33
  40.8 1.6 collective-permute-start.3
  42.5 1.6 collective-permute-start.8
  44.1 1.2 copy-done.24
  45.4 0.7 copy-done.34
  46.1 1.3 slopes.8
  47.4 1.0 join.3.q_ref.refs_15_.refs_7_
  48.6 1.3 slopes.15
  50.1 3.3 %collective-permute-start.4 = (bf16[256,768]{1,0:T(8,128)(2,1)}, bf16[256,768]{1,0:T(8,128)(2,1)S(1)}, u32[]{:S(2)}, u32[]{:S(2)}) collective-permute-start(bf16[256,768]{1,0:T(8,128)(2,1)} %collective-permute-done.3.q_ref.refs_11_.refs_3_), channel_id=1, source_target_pairs={{0,8},{8,0},{16,24},{24,16},{32,40},{40,32},{48,56},{56,48},{64,72... | collective-permute-start | bytes 1179656 | tf_op jit(solution)/shard_map/ppermute | solution.py:55
  53.5 0.6 collective-permute-done.1.q_ref.refs_9_.refs_1_
  54.1 2.3 %slopes.13 = (bf16[2048,256]{1,0:T(8,128)(2,1)S(1)}, f32[1,256]{1,0:T(1,128)S(1)}) custom-call(bf16[256,768]{1,0:T(8,128)(2,1)} %collective-permute-done.5.q_ref.refs_13_.refs_5_, bf16[2048,768]{1,0:T(8,128)(2,1)S(1)} %copy-done, bf16[2048,256]{1,0:T(8,128)(2,1)S(1)} %copy-done.20, f32[1,256]{1,0:T(1,128)S(1)} %copy-done.30), custom_call_target="tpu_custom_call" | custom-call | flops 1200000000 | bytes 150000 | tf_op jit(solution)/shard_map/slopes/pallas_call | solution.py:80
  56.4 2.4 %slopes.11 = (bf16[2048,256]{1,0:T(8,128)(2,1)S(1)}, f32[1,256]{1,0:T(1,128)S(1)}) custom-call(bf16[256,768]{1,0:T(8,128)(2,1)} %collective-permute-done.3.q_ref.refs_11_.refs_3_, bf16[2048,768]{1,0:T(8,128)(2,1)S(1)} %copy-done, bf16[2048,256]{1,0:T(8,128)(2,1)S(1)} %copy-done.18, f32[1,256]{1,0:T(1,128)S(1)} %copy-done.28), custom_call_target="tpu_custom_call" | custom-call | flops 1200000000 | bytes 150000 | tf_op jit(solution)/shard_map/slopes/pallas_call | solution.py:80
  58.9 2.4 %slopes.9 = (bf16[2048,256]{1,0:T(8,128)(2,1)S(1)}, f32[1,256]{1,0:T(1,128)S(1)}) custom-call(bf16[256,768]{1,0:T(8,128)(2,1)} %collective-permute-done.1.q_ref.refs_9_.refs_1_, bf16[2048,768]{1,0:T(8,128)(2,1)S(1)} %copy-done, bf16[2048,256]{1,0:T(8,128)(2,1)S(1)} %copy-done.16, f32[1,256]{1,0:T(1,128)S(1)} %copy-done.26), custom_call_target="tpu_custom_call" | custom-call | flops 1200000000 | bytes 150000 | tf_op jit(solution)/shard_map/slopes/pallas_call | solution.py:80
  61.4 1.4 slopes.14
  62.8 1.3 slopes.12
  64.1 1.3 slopes.10
  65.5 4.7 %class_blocks.2 = (bf16[256,768]{1,0:T(8,128)(2,1)S(1)}, bf16[256,768]{1,0:T(8,128)(2,1)S(1)}, bf16[256,768]{1,0:T(8,128)(2,1)S(1)}, bf16[256,768]{1,0:T(8,128)(2,1)S(1)}) custom-call(s32[4]{0:T(128)S(1)} %pad_add_fusion.1.order_ref, bf16[2048,256]{1,0:T(8,128)(2,1)S(1)} %get-tuple-element.64.refs_0_.s_ref, ...), custom_call_target="tpu_custom_call" | custom-call | flops 2800000000 | bytes 350000 | tf_op jit(solution)/shard_map/class_blocks/pallas_call | solution.py:80
  70.2 4.7 %class_blocks.3 = (bf16[256,768]{1,0:T(8,128)(2,1)S(1)}, bf16[256,768]{1,0:T(8,128)(2,1)S(1)}, bf16[256,768]{1,0:T(8,128)(2,1)S(1)}, bf16[256,768]{1,0:T(8,128)(2,1)S(1)}) custom-call(s32[4]{0:T(128)S(1)} %pad_add_fusion.order_ref, bf16[2048,256]{1,0:T(8,128)(2,1)S(1)} %get-tuple-element.64.refs_0_.s_ref, ...), custom_call_target="tpu_custom_call" | custom-call | flops 2800000000 | bytes 350000 | tf_op jit(solution)/shard_map/class_blocks/pallas_call | solution.py:80
  74.9 3.7 %give.1 = (bf16[2,144,768]{2,1,0:T(8,128)(2,1)S(1)}, bf16[2,144,768]{2,1,0:T(8,128)(2,1)S(1)}, bf16[2,144,768]{2,1,0:T(8,128)(2,1)S(1)}, bf16[144,768]{1,0:T(8,128)(2,1)S(1)}, bf16[144,768]{1,0:T(8,128)(2,1)S(1)}) custom-call(s32[1]{0:T(128)} %bitcast.me_ref, bf16[2048,768]{1,0:T(8,128)(2,1)S(1)} %copy-done, ...), custom_call_target="tpu_custom_call" | custom-call | flops 3600000000 | bytes 450000 | tf_op jit(solution)/shard_map/give/pallas_call | solution.py:80
  78.6 0.6 collective-permute-start.10
  79.8 2.4 %collective-permute-done.12.r7 = bf16[144,768]{1,0:T(8,128)(2,1)S(1)} collective-permute-done((bf16[144,768]{1,0:T(8,128)(2,1)S(1)}, bf16[144,768]{1,0:T(8,128)(2,1)S(1)}, u32[]{:S(2)}, u32[]{:S(2)}) %collective-permute-start.12) | collective-permute-done | bytes 221216 | tf_op jit(solution)/shard_map/ppermute | solution.py:55
  82.2 2.8 %take.1 = (bf16[2,144,768]{2,1,0:T(8,128)(2,1)S(1)}, bf16[2,144,768]{2,1,0:T(8,128)(2,1)S(1)}, bf16[2,144,768]{2,1,0:T(8,128)(2,1)S(1)}, bf16[144,768]{1,0:T(8,128)(2,1)S(1)}) custom-call(bf16[2048,768]{1,0:T(8,128)(2,1)S(1)} %copy-done, bf16[2048,256]{1,0:T(8,128)(2,1)S(1)} %get-tuple-element.67.refs_1_.s1, ...), custom_call_target="tpu_custom_call" | custom-call | flops 3200000000 | bytes 400000 | tf_op jit(solution)/shard_map/take/pallas_call | solution.py:80
  85.0 2.4 %collective-permute-start.13 = (bf16[2,144,768]{2,1,0:T(8,128)(2,1)S(1)}, bf16[2,144,768]{2,1,0:T(8,128)(2,1)S(1)}, u32[]{:S(2)}, u32[]{:S(2)}) collective-permute-start(bf16[2,144,768]{2,1,0:T(8,128)(2,1)S(1)} %get-tuple-element.104), channel_id=1, source_target_pairs={{0,96},{8,40},{16,112},{24,56},{32,0},{40,72},{48,16},{56,88},{64,... | collective-permute-start | bytes 1327112 | tf_op jit(solution)/shard_map/ppermute | solution.py:55
  87.4 1.1 collective-permute-start.14
  88.5 2.1 %collective-permute-start.15 = (bf16[2,144,768]{2,1,0:T(8,128)(2,1)S(1)}, bf16[2,144,768]{2,1,0:T(8,128)(2,1)S(1)}, u32[]{:S(2)}, u32[]{:S(2)}) collective-permute-start(bf16[2,144,768]{2,1,0:T(8,128)(2,1)S(1)} %get-tuple-element.106), channel_id=1, source_target_pairs={{0,112},{8,56},{16,96},{24,40},{32,16},{40,88},{48,0},{56,72},{64,... | collective-permute-start | bytes 1327112 | tf_op jit(solution)/shard_map/ppermute | solution.py:55
  90.6 1.5 collective-permute-start.22
  92.1 1.7 %collective-permute-start.23 = (bf16[256,768]{1,0:T(8,128)(2,1)S(1)}, bf16[256,768]{1,0:T(8,128)(2,1)S(1)}, u32[]{:S(2)}, u32[]{:S(2)}) collective-permute-start(bf16[256,768]{1,0:T(8,128)(2,1)S(1)} %get-tuple-element.116), channel_id=1, source_target_pairs={{0,3},{1,0},{2,1},{3,2},{4,7},{5,4},{6,5},{7,6},{8,11},{9,8},{10,9... | collective-permute-start | bytes 1179656 | tf_op jit(solution)/shard_map/ppermute | solution.py:432
  93.8 7.7 %collective-permute-done.22 = bf16[256,768]{1,0:T(8,128)(2,1)S(1)} collective-permute-done((bf16[256,768]{1,0:T(8,128)(2,1)S(1)}, bf16[256,768]{1,0:T(8,128)(2,1)S(1)}, u32[]{:S(2)}, u32[]{:S(2)}) %collective-permute-start.22) | collective-permute-done | bytes 393248 | tf_op jit(solution)/shard_map/ppermute | solution.py:432
  101.5 4.0 %collective-permute-start.18 = (bf16[256,768]{1,0:T(8,128)(2,1)S(1)}, bf16[256,768]{1,0:T(8,128)(2,1)S(1)}, u32[]{:S(2)}, u32[]{:S(2)}) collective-permute-start(bf16[256,768]{1,0:T(8,128)(2,1)S(1)} %get-tuple-element.86), channel_id=1, source_target_pairs={{0,6},{1,7},{2,4},{3,5},{4,2},{5,3},{6,0},{7,1},{8,14},{9,15},{10,... | collective-permute-start | bytes 1179656 | tf_op jit(solution)/shard_map/ppermute | solution.py:432
  105.5 0.5 collective-permute-start.24
  106.1 3.0 %collective-permute-start.19 = (bf16[256,768]{1,0:T(8,128)(2,1)S(1)}, bf16[256,768]{1,0:T(8,128)(2,1)S(1)}, u32[]{:S(2)}, u32[]{:S(2)}) collective-permute-start(bf16[256,768]{1,0:T(8,128)(2,1)S(1)} %get-tuple-element.112), channel_id=1, source_target_pairs={{0,5},{1,6},{2,7},{3,4},{4,1},{5,2},{6,3},{7,0},{8,13},{9,14},{10,... | collective-permute-start | bytes 1179656 | tf_op jit(solution)/shard_map/ppermute | solution.py:432
  109.1 2.6 %collective-permute-start.20 = (bf16[256,768]{1,0:T(8,128)(2,1)S(1)}, bf16[256,768]{1,0:T(8,128)(2,1)S(1)}, u32[]{:S(2)}, u32[]{:S(2)}) collective-permute-start(bf16[256,768]{1,0:T(8,128)(2,1)S(1)} %get-tuple-element.113), channel_id=1, source_target_pairs={{0,7},{1,4},{2,5},{3,6},{4,3},{5,0},{6,1},{7,2},{8,15},{9,12},{10,... | collective-permute-start | bytes 1179656 | tf_op jit(solution)/shard_map/ppermute | solution.py:432
  111.7 21.2 %collective-permute-start.21 = (bf16[256,768]{1,0:T(8,128)(2,1)S(1)}, bf16[256,768]{1,0:T(8,128)(2,1)S(1)}, u32[]{:S(2)}, u32[]{:S(2)}) collective-permute-start(bf16[256,768]{1,0:T(8,128)(2,1)S(1)} %get-tuple-element.114), channel_id=1, source_target_pairs={{0,2},{1,3},{2,0},{3,1},{4,6},{5,7},{6,4},{7,5},{8,10},{9,11},{10,... | collective-permute-start | bytes 1179656 | tf_op jit(solution)/shard_map/ppermute | solution.py:432
  132.9 1.0 own.1
  134.2 6.6 %collective-permute-done.24 = bf16[256,768]{1,0:T(8,128)(2,1)S(1)} collective-permute-done((bf16[256,768]{1,0:T(8,128)(2,1)S(1)}, bf16[256,768]{1,0:T(8,128)(2,1)S(1)}, u32[]{:S(2)}, u32[]{:S(2)}) %collective-permute-start.24) | collective-permute-done | bytes 393248 | tf_op jit(solution)/shard_map/ppermute | solution.py:432
  140.8 3.7 %collective-permute-start.17 = (bf16[144,768]{1,0:T(8,128)(2,1)S(1)}, bf16[144,768]{1,0:T(8,128)(2,1)S(1)}, u32[]{:S(2)}, u32[]{:S(2)}) collective-permute-start(bf16[144,768]{1,0:T(8,128)(2,1)S(1)} %get-tuple-element.109), channel_id=1, source_target_pairs={{0,80},{8,88},{16,64},{24,72},{32,112},{40,120},{48,96},{56,104},{... | collective-permute-start | bytes 663560 | tf_op jit(solution)/shard_map/ppermute | solution.py:55
  144.6 1.2 add_convert_fusion
  145.8 4.5 %collective-permute-done.17.far = bf16[144,768]{1,0:T(8,128)(2,1)S(1)} collective-permute-done((bf16[144,768]{1,0:T(8,128)(2,1)S(1)}, bf16[144,768]{1,0:T(8,128)(2,1)S(1)}, u32[]{:S(2)}, u32[]{:S(2)}) %collective-permute-start.17) | collective-permute-done | bytes 221216 | tf_op jit(solution)/shard_map/ppermute | solution.py:55
  150.3 0.8 finish.1
  151.1 1.3 copy-done.37
  152.4 6.4 %bounds.1 = f32[1,2048]{1,0:T(1,128)} custom-call(s32[1]{0:T(128)} %bitcast.me_ref, bf16[16,48,768]{2,1,0:T(8,128)(2,1)S(1)} %bitcast.21, bf16[256,768]{1,0:T(8,128)(2,1)S(1)} %join.2.q_ref.refs_8_.refs_0_, bf16[256,768]{1,0:T(8,128)(2,1)} %collective-permute-done.1.q_ref.refs_9_.refs_1_, bf16[256,768]{1,0:T(8,128)(2,1)S(1)} %copy-done.8, ...), custom_call_target="tpu_custom_call" | custom-call | flops 3200000000 | bytes 400000 | tf_op jit(solution)/shard_map/bounds/pallas_call | solution.py:80
  (108 shorter events, 2.2 us)
Async XLA Ops:
  7.2 143.9 %all-gather.3.cloned.1.call-start = ((), (), s32[]{:S(2)}) async-start(), calls=%async_computation | async-start | bytes 1253376 | tf_op jit(solution)/shard_map/all_gather | solution.py:406
  7.9 2.3 %copy-start.35 = (bf16[768,3072]{1,0:T(8,128)(2,1)S(1)}, bf16[768,3072]{1,0:T(8,128)(2,1)}, u32[]{:S(2)}) copy-start(bf16[768,3072]{1,0:T(8,128)(2,1)} %w_in_ref.1) | copy-start | bytes 14155780
  10.2 2.3 %copy-start.36 = (bf16[3072,768]{1,0:T(8,128)(2,1)S(1)}, bf16[3072,768]{1,0:T(8,128)(2,1)}, u32[]{:S(2)}) copy-start(bf16[3072,768]{1,0:T(8,128)(2,1)} %w_out_ref.1) | copy-start | bytes 14155780
  12.6 0.9 copy-start.38
  13.5 8.4 %copy-start.43 = (f32[32]{0:T(128)S(1)}, f32[32]{0:T(128)}, u32[]{:S(2)}) copy-start(f32[32]{0:T(128)} %param.16) | copy-start | bytes 388
  13.5 8.6 %copy-start.42 = (bf16[32,768]{1,0:T(8,128)(2,1)S(1)}, bf16[32,768]{1,0:T(8,128)(2,1)}, u32[]{:S(2)}) copy-start(bf16[32,768]{1,0:T(8,128)(2,1)} %param.15) | copy-start | bytes 147460
  16.9 5.8 %collective-permute-start = (bf16[128,768]{1,0:T(8,128)(2,1)}, bf16[128,768]{1,0:T(8,128)(2,1)S(1)}, u32[]{:S(2)}, u32[]{:S(2)}) collective-permute-start(bf16[128,768]{1,0:T(8,128)(2,1)} %encode.1.own_ref), channel_id=1, source_target_pairs={{0,8},{8,0},{16,24},{24,16},{32,40},{40,32},{48,56},{56,48},{64,72... | collective-permute-start | bytes 589832 | tf_op jit(solution)/shard_map/ppermute | solution.py:55
  16.9 25.6 %collective-permute-start.7 = (bf16[128,768]{1,0:T(8,128)(2,1)}, bf16[128,768]{1,0:T(8,128)(2,1)}, u32[]{:S(2)}, u32[]{:S(2)}) collective-permute-start(bf16[128,768]{1,0:T(8,128)(2,1)} %encode.1.own_ref), channel_id=1, source_target_pairs={{0,80},{8,88},{16,64},{24,72},{32,112},{40,120},{48,96},{56,104},{... | collective-permute-start | bytes 589832 | tf_op jit(solution)/shard_map/ppermute | solution.py:55
  23.7 24.7 %collective-permute-start.5 = (bf16[256,768]{1,0:T(8,128)(2,1)S(1)}, bf16[256,768]{1,0:T(8,128)(2,1)}, u32[]{:S(2)}, u32[]{:S(2)}) collective-permute-start(bf16[256,768]{1,0:T(8,128)(2,1)S(1)} %join.2.q_ref.refs_8_.refs_0_), channel_id=1, source_target_pairs={{0,48},{8,120},{16,32},{24,104},{32,80},{40,24},{48,64},{56,8},{64... | collective-permute-start | bytes 1179656 | tf_op jit(solution)/shard_map/ppermute | solution.py:55
  24.7 0.9 copy-start.39
  25.6 0.8 copy-start.40
  27.0 17.1 %copy-start = (bf16[2048,768]{1,0:T(8,128)(2,1)S(1)}, bf16[2048,768]{1,0:T(8,128)(2,1)}, u32[]{:S(2)}) copy-start(bf16[2048,768]{1,0:T(8,128)(2,1)} %c_ref.21) | copy-start | bytes 9437188
  30.6 1.0 copy-start.9
  31.6 1.0 copy-start.11
  32.6 1.0 copy-start.13
  33.6 1.0 copy-start.15
  34.6 1.0 copy-start.17
  35.6 1.1 copy-start.19
  36.6 1.0 copy-start.21
  37.7 1.0 copy-start.23
  40.8 1.6 copy-start.31
  40.8 9.3 %collective-permute-start.3 = (bf16[256,768]{1,0:T(8,128)(2,1)S(1)}, bf16[256,768]{1,0:T(8,128)(2,1)}, u32[]{:S(2)}, u32[]{:S(2)}) collective-permute-start(bf16[256,768]{1,0:T(8,128)(2,1)S(1)} %join.2.q_ref.refs_8_.refs_0_), channel_id=1, source_target_pairs={{0,16},{8,72},{16,0},{24,88},{32,48},{40,104},{48,32},{56,120},{64... | collective-permute-start | bytes 1179656 | tf_op jit(solution)/shard_map/ppermute | solution.py:55
  42.4 11.6 %collective-permute-start.1 = (bf16[256,768]{1,0:T(8,128)(2,1)S(1)}, bf16[256,768]{1,0:T(8,128)(2,1)}, u32[]{:S(2)}, u32[]{:S(2)}) collective-permute-start(bf16[256,768]{1,0:T(8,128)(2,1)S(1)} %join.2.q_ref.refs_8_.refs_0_), channel_id=1, source_target_pairs={{0,32},{8,104},{16,48},{24,120},{32,64},{40,8},{48,80},{56,24},{64... | collective-permute-start | bytes 1179656 | tf_op jit(solution)/shard_map/ppermute | solution.py:55
  42.5 6.1 %copy-start.22 = (bf16[2048,256]{1,0:T(8,128)(2,1)S(1)}, bf16[2048,256]{1,0:T(8,128)(2,1)}, u32[]{:S(2)}) copy-start(bf16[2048,256]{1,0:T(8,128)(2,1)} %copy-done.21) | copy-start | bytes 3145732
  42.5 4.9 %collective-permute-start.8 = (bf16[128,768]{1,0:T(8,128)(2,1)}, bf16[128,768]{1,0:T(8,128)(2,1)S(1)}, u32[]{:S(2)}, u32[]{:S(2)}) collective-permute-start(bf16[128,768]{1,0:T(8,128)(2,1)} %collective-permute-done.7.own_ref), channel_id=1, source_target_pairs={{0,8},{8,0},{16,24},{24,16},{32,40},{40,32},{48,56},{56,48},{64,72... | collective-permute-start | bytes 589832 | tf_op jit(solution)/shard_map/ppermute | solution.py:55
  44.1 1.2 copy-start.24
  46.1 2.6 %copy-start.32 = (f32[1,256]{1,0:T(1,128)S(1)}, f32[1,256]{1,0:T(1,128)}, u32[]{:S(2)}) copy-start(f32[1,256]{1,0:T(1,128)} %copy-done.31) | copy-start | bytes 3076
  46.1 8.0 %copy-start.20 = (bf16[2048,256]{1,0:T(8,128)(2,1)S(1)}, bf16[2048,256]{1,0:T(8,128)(2,1)}, u32[]{:S(2)}) copy-start(bf16[2048,256]{1,0:T(8,128)(2,1)} %copy-done.19) | copy-start | bytes 3145732
  46.1 8.0 %copy-start.30 = (f32[1,256]{1,0:T(1,128)S(1)}, f32[1,256]{1,0:T(1,128)}, u32[]{:S(2)}) copy-start(f32[1,256]{1,0:T(1,128)} %copy-done.29) | copy-start | bytes 3076
  48.4 21.8 %copy-start.1 = (bf16[256,768]{1,0:T(8,128)(2,1)}, bf16[256,768]{1,0:T(8,128)(2,1)S(1)}, u32[]{:S(2)}) copy-start(bf16[256,768]{1,0:T(8,128)(2,1)S(1)} %join.3.q_ref.refs_15_.refs_7_) | copy-start | bytes 1179652
  48.4 8.0 %copy-start.18 = (bf16[2048,256]{1,0:T(8,128)(2,1)S(1)}, bf16[2048,256]{1,0:T(8,128)(2,1)}, u32[]{:S(2)}) copy-start(bf16[2048,256]{1,0:T(8,128)(2,1)} %copy-done.17) | copy-start | bytes 3145732
  48.4 8.0 %copy-start.28 = (f32[1,256]{1,0:T(1,128)S(1)}, f32[1,256]{1,0:T(1,128)}, u32[]{:S(2)}) copy-start(f32[1,256]{1,0:T(1,128)} %copy-done.27) | copy-start | bytes 3076
  48.4 12.9 %collective-permute-start.6 = (bf16[256,768]{1,0:T(8,128)(2,1)}, bf16[256,768]{1,0:T(8,128)(2,1)S(1)}, u32[]{:S(2)}, u32[]{:S(2)}) collective-permute-start(bf16[256,768]{1,0:T(8,128)(2,1)} %collective-permute-done.5.q_ref.refs_13_.refs_5_), channel_id=1, source_target_pairs={{0,8},{8,0},{16,24},{24,16},{32,40},{40,32},{48,56},{56,48},{64,72... | collective-permute-start | bytes 1179656 | tf_op jit(solution)/shard_map/ppermute | solution.py:55
  50.0 8.9 %copy-start.16 = (bf16[2048,256]{1,0:T(8,128)(2,1)S(1)}, bf16[2048,256]{1,0:T(8,128)(2,1)}, u32[]{:S(2)}) copy-start(bf16[2048,256]{1,0:T(8,128)(2,1)} %copy-done.15) | copy-start | bytes 3145732
  50.0 8.9 %copy-start.26 = (f32[1,256]{1,0:T(1,128)S(1)}, f32[1,256]{1,0:T(1,128)}, u32[]{:S(2)}) copy-start(f32[1,256]{1,0:T(1,128)} %copy-done.25) | copy-start | bytes 3076
  50.1 12.6 %collective-permute-start.4 = (bf16[256,768]{1,0:T(8,128)(2,1)}, bf16[256,768]{1,0:T(8,128)(2,1)S(1)}, u32[]{:S(2)}, u32[]{:S(2)}) collective-permute-start(bf16[256,768]{1,0:T(8,128)(2,1)} %collective-permute-done.3.q_ref.refs_11_.refs_3_), channel_id=1, source_target_pairs={{0,8},{8,0},{16,24},{24,16},{32,40},{40,32},{48,56},{56,48},{64,72... | collective-permute-start | bytes 1179656 | tf_op jit(solution)/shard_map/ppermute | solution.py:55
  54.0 10.1 %collective-permute-start.2 = (bf16[256,768]{1,0:T(8,128)(2,1)}, bf16[256,768]{1,0:T(8,128)(2,1)S(1)}, u32[]{:S(2)}, u32[]{:S(2)}) collective-permute-start(bf16[256,768]{1,0:T(8,128)(2,1)} %collective-permute-done.1.q_ref.refs_9_.refs_1_), channel_id=1, source_target_pairs={{0,8},{8,0},{16,24},{24,16},{32,40},{40,32},{48,56},{56,48},{64,72... | collective-permute-start | bytes 1179656 | tf_op jit(solution)/shard_map/ppermute | solution.py:55
  56.4 5.0 %copy-start.14 = (bf16[2048,256]{1,0:T(8,128)(2,1)S(1)}, bf16[2048,256]{1,0:T(8,128)(2,1)}, u32[]{:S(2)}) copy-start(bf16[2048,256]{1,0:T(8,128)(2,1)} %copy-done.13) | copy-start | bytes 3145732
  58.9 3.9 %copy-start.12 = (bf16[2048,256]{1,0:T(8,128)(2,1)S(1)}, bf16[2048,256]{1,0:T(8,128)(2,1)}, u32[]{:S(2)}) copy-start(bf16[2048,256]{1,0:T(8,128)(2,1)} %copy-done.11) | copy-start | bytes 3145732
  61.3 2.8 %copy-start.10 = (bf16[2048,256]{1,0:T(8,128)(2,1)S(1)}, bf16[2048,256]{1,0:T(8,128)(2,1)}, u32[]{:S(2)}) copy-start(bf16[2048,256]{1,0:T(8,128)(2,1)} %copy-done.9) | copy-start | bytes 3145732
  61.4 8.8 %copy-start.3 = (bf16[256,768]{1,0:T(8,128)(2,1)}, bf16[256,768]{1,0:T(8,128)(2,1)S(1)}, u32[]{:S(2)}) copy-start(bf16[256,768]{1,0:T(8,128)(2,1)S(1)} %collective-permute-done.6.q_ref.refs_14_.refs_6_) | copy-start | bytes 1179652
  62.7 7.4 %copy-start.5 = (bf16[256,768]{1,0:T(8,128)(2,1)}, bf16[256,768]{1,0:T(8,128)(2,1)S(1)}, u32[]{:S(2)}) copy-start(bf16[256,768]{1,0:T(8,128)(2,1)S(1)} %collective-permute-done.4.q_ref.refs_12_.refs_4_) | copy-start | bytes 1179652
  64.1 6.1 %copy-start.7 = (bf16[256,768]{1,0:T(8,128)(2,1)}, bf16[256,768]{1,0:T(8,128)(2,1)S(1)}, u32[]{:S(2)}) copy-start(bf16[256,768]{1,0:T(8,128)(2,1)S(1)} %collective-permute-done.2.q_ref.refs_10_.refs_2_) | copy-start | bytes 1179652
  78.6 3.6 %collective-permute-start.10 = (bf16[2,144,768]{2,1,0:T(8,128)(2,1)S(1)}, bf16[2,144,768]{2,1,0:T(8,128)(2,1)S(1)}, u32[]{:S(2)}, u32[]{:S(2)}) collective-permute-start(bf16[2,144,768]{2,1,0:T(8,128)(2,1)S(1)} %get-tuple-element.101), channel_id=1, source_target_pairs={{0,8},{8,0},{16,24},{24,16},{32,40},{40,32},{48,56},{56,48},{64,72... | collective-permute-start | bytes 1327112 | tf_op jit(solution)/shard_map/ppermute | solution.py:55
  79.2 3.0 %collective-permute-start.11 = (bf16[2,144,768]{2,1,0:T(8,128)(2,1)S(1)}, bf16[2,144,768]{2,1,0:T(8,128)(2,1)S(1)}, u32[]{:S(2)}, u32[]{:S(2)}) collective-permute-start(bf16[2,144,768]{2,1,0:T(8,128)(2,1)S(1)} %get-tuple-element.102), channel_id=1, source_target_pairs={{0,8},{8,0},{16,24},{24,16},{32,40},{40,32},{48,56},{56,48},{64,72... | collective-permute-start | bytes 1327112 | tf_op jit(solution)/shard_map/ppermute | solution.py:55
  79.3 2.9 %collective-permute-start.9 = (bf16[2,144,768]{2,1,0:T(8,128)(2,1)S(1)}, bf16[2,144,768]{2,1,0:T(8,128)(2,1)S(1)}, u32[]{:S(2)}, u32[]{:S(2)}) collective-permute-start(bf16[2,144,768]{2,1,0:T(8,128)(2,1)S(1)} %get-tuple-element.100), channel_id=1, source_target_pairs={{0,8},{8,0},{16,24},{24,16},{32,40},{40,32},{48,56},{56,48},{64,72... | collective-permute-start | bytes 1327112 | tf_op jit(solution)/shard_map/ppermute | solution.py:55
  79.7 2.5 %collective-permute-start.12 = (bf16[144,768]{1,0:T(8,128)(2,1)S(1)}, bf16[144,768]{1,0:T(8,128)(2,1)S(1)}, u32[]{:S(2)}, u32[]{:S(2)}) collective-permute-start(bf16[144,768]{1,0:T(8,128)(2,1)S(1)} %get-tuple-element.94), channel_id=1, source_target_pairs={{0,8},{8,0},{16,24},{24,16},{32,40},{40,32},{48,56},{56,48},{64,72... | collective-permute-start | bytes 663560 | tf_op jit(solution)/shard_map/ppermute | solution.py:55
  85.0 21.1 %collective-permute-start.13 = (bf16[2,144,768]{2,1,0:T(8,128)(2,1)S(1)}, bf16[2,144,768]{2,1,0:T(8,128)(2,1)S(1)}, u32[]{:S(2)}, u32[]{:S(2)}) collective-permute-start(bf16[2,144,768]{2,1,0:T(8,128)(2,1)S(1)} %get-tuple-element.104), channel_id=1, source_target_pairs={{0,96},{8,40},{16,112},{24,56},{32,0},{40,72},{48,16},{56,88},{64,... | collective-permute-start | bytes 1327112 | tf_op jit(solution)/shard_map/ppermute | solution.py:55
  87.4 21.7 %collective-permute-start.14 = (bf16[2,144,768]{2,1,0:T(8,128)(2,1)S(1)}, bf16[2,144,768]{2,1,0:T(8,128)(2,1)S(1)}, u32[]{:S(2)}, u32[]{:S(2)}) collective-permute-start(bf16[2,144,768]{2,1,0:T(8,128)(2,1)S(1)} %get-tuple-element.105), channel_id=1, source_target_pairs={{0,16},{8,72},{16,0},{24,88},{32,48},{40,104},{48,32},{56,120},{64... | collective-permute-start | bytes 1327112 | tf_op jit(solution)/shard_map/ppermute | solution.py:55
  88.5 23.2 %collective-permute-start.15 = (bf16[2,144,768]{2,1,0:T(8,128)(2,1)S(1)}, bf16[2,144,768]{2,1,0:T(8,128)(2,1)S(1)}, u32[]{:S(2)}, u32[]{:S(2)}) collective-permute-start(bf16[2,144,768]{2,1,0:T(8,128)(2,1)S(1)} %get-tuple-element.106), channel_id=1, source_target_pairs={{0,112},{8,56},{16,96},{24,40},{32,16},{40,88},{48,0},{56,72},{64,... | collective-permute-start | bytes 1327112 | tf_op jit(solution)/shard_map/ppermute | solution.py:55
  90.6 10.9 %collective-permute-start.22 = (bf16[256,768]{1,0:T(8,128)(2,1)S(1)}, bf16[256,768]{1,0:T(8,128)(2,1)S(1)}, u32[]{:S(2)}, u32[]{:S(2)}) collective-permute-start(bf16[256,768]{1,0:T(8,128)(2,1)S(1)} %get-tuple-element.115), channel_id=1, source_target_pairs={{0,1},{1,2},{2,3},{3,0},{4,5},{5,6},{6,7},{7,4},{8,9},{9,10},{10,1... | collective-permute-start | bytes 1179656 | tf_op jit(solution)/shard_map/ppermute | solution.py:432
  92.1 13.5 %collective-permute-start.23 = (bf16[256,768]{1,0:T(8,128)(2,1)S(1)}, bf16[256,768]{1,0:T(8,128)(2,1)S(1)}, u32[]{:S(2)}, u32[]{:S(2)}) collective-permute-start(bf16[256,768]{1,0:T(8,128)(2,1)S(1)} %get-tuple-element.116), channel_id=1, source_target_pairs={{0,3},{1,0},{2,1},{3,2},{4,7},{5,4},{6,5},{7,6},{8,11},{9,8},{10,9... | collective-permute-start | bytes 1179656 | tf_op jit(solution)/shard_map/ppermute | solution.py:432
  101.5 43.1 %collective-permute-start.18 = (bf16[256,768]{1,0:T(8,128)(2,1)S(1)}, bf16[256,768]{1,0:T(8,128)(2,1)S(1)}, u32[]{:S(2)}, u32[]{:S(2)}) collective-permute-start(bf16[256,768]{1,0:T(8,128)(2,1)S(1)} %get-tuple-element.86), channel_id=1, source_target_pairs={{0,6},{1,7},{2,4},{3,5},{4,2},{5,3},{6,0},{7,1},{8,14},{9,15},{10,... | collective-permute-start | bytes 1179656 | tf_op jit(solution)/shard_map/ppermute | solution.py:432
  105.5 35.3 %collective-permute-start.24 = (bf16[256,768]{1,0:T(8,128)(2,1)S(1)}, bf16[256,768]{1,0:T(8,128)(2,1)S(1)}, u32[]{:S(2)}, u32[]{:S(2)}) collective-permute-start(bf16[256,768]{1,0:T(8,128)(2,1)S(1)} %get-tuple-element.117), channel_id=1, source_target_pairs={{0,4},{1,5},{2,6},{3,7},{4,0},{5,1},{6,2},{7,3},{8,12},{9,13},{10,... | collective-permute-start | bytes 1179656 | tf_op jit(solution)/shard_map/ppermute | solution.py:432
  106.1 38.5 %collective-permute-start.19 = (bf16[256,768]{1,0:T(8,128)(2,1)S(1)}, bf16[256,768]{1,0:T(8,128)(2,1)S(1)}, u32[]{:S(2)}, u32[]{:S(2)}) collective-permute-start(bf16[256,768]{1,0:T(8,128)(2,1)S(1)} %get-tuple-element.112), channel_id=1, source_target_pairs={{0,5},{1,6},{2,7},{3,4},{4,1},{5,2},{6,3},{7,0},{8,13},{9,14},{10,... | collective-permute-start | bytes 1179656 | tf_op jit(solution)/shard_map/ppermute | solution.py:432
  109.1 35.5 %collective-permute-start.20 = (bf16[256,768]{1,0:T(8,128)(2,1)S(1)}, bf16[256,768]{1,0:T(8,128)(2,1)S(1)}, u32[]{:S(2)}, u32[]{:S(2)}) collective-permute-start(bf16[256,768]{1,0:T(8,128)(2,1)S(1)} %get-tuple-element.113), channel_id=1, source_target_pairs={{0,7},{1,4},{2,5},{3,6},{4,3},{5,0},{6,1},{7,2},{8,15},{9,12},{10,... | collective-permute-start | bytes 1179656 | tf_op jit(solution)/shard_map/ppermute | solution.py:432
  111.7 32.9 %collective-permute-start.21 = (bf16[256,768]{1,0:T(8,128)(2,1)S(1)}, bf16[256,768]{1,0:T(8,128)(2,1)S(1)}, u32[]{:S(2)}, u32[]{:S(2)}) collective-permute-start(bf16[256,768]{1,0:T(8,128)(2,1)S(1)} %get-tuple-element.114), channel_id=1, source_target_pairs={{0,2},{1,3},{2,0},{3,1},{4,6},{5,7},{6,4},{7,5},{8,10},{9,11},{10,... | collective-permute-start | bytes 1179656 | tf_op jit(solution)/shard_map/ppermute | solution.py:432
  134.0 17.1 %copy-start.2 = (bf16[256,768]{1,0:T(8,128)(2,1)S(1)}, bf16[256,768]{1,0:T(8,128)(2,1)}, u32[]{:S(2)}) copy-start(bf16[256,768]{1,0:T(8,128)(2,1)} %copy-done.1) | copy-start | bytes 1179652
  134.0 17.1 %copy-start.4 = (bf16[256,768]{1,0:T(8,128)(2,1)S(1)}, bf16[256,768]{1,0:T(8,128)(2,1)}, u32[]{:S(2)}) copy-start(bf16[256,768]{1,0:T(8,128)(2,1)} %copy-done.3) | copy-start | bytes 1179652
  134.0 17.1 %copy-start.6 = (bf16[256,768]{1,0:T(8,128)(2,1)S(1)}, bf16[256,768]{1,0:T(8,128)(2,1)}, u32[]{:S(2)}) copy-start(bf16[256,768]{1,0:T(8,128)(2,1)} %copy-done.5) | copy-start | bytes 1179652
  134.0 17.1 %copy-start.8 = (bf16[256,768]{1,0:T(8,128)(2,1)S(1)}, bf16[256,768]{1,0:T(8,128)(2,1)}, u32[]{:S(2)}) copy-start(bf16[256,768]{1,0:T(8,128)(2,1)} %copy-done.7) | copy-start | bytes 1179652
  140.8 9.5 %collective-permute-start.17 = (bf16[144,768]{1,0:T(8,128)(2,1)S(1)}, bf16[144,768]{1,0:T(8,128)(2,1)S(1)}, u32[]{:S(2)}, u32[]{:S(2)}) collective-permute-start(bf16[144,768]{1,0:T(8,128)(2,1)S(1)} %get-tuple-element.109), channel_id=1, source_target_pairs={{0,80},{8,88},{16,64},{24,72},{32,112},{40,120},{48,96},{56,104},{... | collective-permute-start | bytes 663560 | tf_op jit(solution)/shard_map/ppermute | solution.py:55
  144.6 5.7 %collective-permute-start.16 = (bf16[144,768]{1,0:T(8,128)(2,1)S(1)}, bf16[144,768]{1,0:T(8,128)(2,1)S(1)}, u32[]{:S(2)}, u32[]{:S(2)}) collective-permute-start(bf16[144,768]{1,0:T(8,128)(2,1)S(1)} %get-tuple-element.108), channel_id=1, source_target_pairs={{0,8},{8,0},{16,24},{24,16},{32,40},{40,32},{48,56},{56,48},{64,72... | collective-permute-start | bytes 663560 | tf_op jit(solution)/shard_map/ppermute | solution.py:55
  151.1 1.3 copy-start.37
  (6 other events, 3.5 us)
Sparse Core Ops, SparseCore 0:
  22.8 35.6 all-gather.2
